TPU v7x, 512 devices: a whole 4x8x8 slice. The times are simulated.
512 devices in a mesh: grp: 8 (over x, core), ef: 64 (over z, y).
Axes of the slice: x: 4, y: 8, z: 8, core: 2. Of those that a mesh axis runs over, the one named last changes fastest.
Arguments:
- amplitudes: bfloat16 [360000, 512], P('ef', 'grp'), may hold values from -6 to 6
- ladder: bfloat16 [2304, 360000], P('grp', 'ef'), may hold values from -0.01953125 to 0.01953125
- orbital_irrep: int32 [600], replicated, may hold values from 0 to 3
- panel_rows: int32 [2304], P('grp'), may hold values from 0 to 359999
- slot_pair: int32 [64], replicated, may hold values from 0 to 63, each once
Outputs:
- sigma_out: float32 [2304, 512], P('grp', 'ef')
Inputs may be any that keep to these rules, and one draw needn't show every extreme that they name: `slot_pair`: each slot holds a different pair.
All inputs are finite; a program needn't handle non-finite values.
Results may differ from a plain program's by a relative error of at most 0.0003.
Values may be sent and summed in bfloat16 or wider, within the bound.
No kernel may reach another device: no remote copies, remote signals or barrier semaphores. Data moves between devices by JAX's collectives and lax.ppermute only.
A program may use at most 64 MiB of HBM per device.

v0:
```python
import jax
import jax.numpy as jnp
from jax import lax
from jax.sharding import PartitionSpec as P

V = 600


def lookup(indices, orbital_irrep):
    orbitals = jnp.arange(orbital_irrep.shape[0], dtype=jnp.int32)
    return jnp.max(
        jnp.where(indices[:, None] == orbitals[None, :], orbital_irrep[None, :], 0), axis=1
    )


def on_device(amplitudes, ladder, orbital_irrep, panel_rows, slot_pair):
    shard_width = ladder.shape[1]
    offset = lax.axis_index("ef") * shard_width
    columns = offset + jnp.arange(shard_width, dtype=jnp.int32)
    col_sym = jnp.bitwise_xor(
        lookup(columns // V, orbital_irrep), lookup(columns % V, orbital_irrep)
    )
    row_sym = jnp.bitwise_xor(
        lookup(panel_rows // V, orbital_irrep), lookup(panel_rows % V, orbital_irrep)
    )
    masked = jnp.where(row_sym[:, None] == col_sym[None, :], ladder, jnp.zeros((), ladder.dtype))
    gathered = lax.all_gather(amplitudes, "grp", axis=1, tiled=True)
    partial_value = jnp.dot(masked, gathered, preferred_element_type=jnp.float32)
    row_count = ladder.shape[0]
    pair_count = slot_pair.shape[0]
    partial_value = partial_value.reshape(row_count, pair_count, -1)
    permuter = (slot_pair[:, None] == jnp.arange(pair_count, dtype=jnp.int32)[None, :]).astype(
        jnp.float32
    )
    ordered = jnp.einsum("asr,sp->apr", partial_value, permuter, precision=lax.Precision.HIGHEST)
    ordered = ordered.reshape(row_count, -1)
    return lax.psum_scatter(ordered, "ef", scatter_dimension=1, tiled=True)


def solution(mesh):
    in_specs = (P("ef", "grp"), P("grp", "ef"), P(), P("grp"), P())
    out_specs = P("grp", "ef")
    return jax.shard_map(
        on_device, mesh=mesh, in_specs=in_specs, out_specs=out_specs, check_vma=False
    )
```

profile of v0, /device:TPU:6, one launch (start us, length us, event | category | flops | bytes accessed | tf_op | source)
XLA Modules:
  0.0 234.0 jit_solution(14535526977654354586)
XLA Ops:
  6.5 0.0 all-gather.2.cloned.1.call-start
  6.5 0.7 all-gather.2.cloned.1.call-update
  7.3 0.0 all-reduce.3.cloned.1.call-start
  7.3 5.8 %select_reduce_fusion = (s32[5625]{0:T(1024)S(1)}, s32[5625]{0:T(1024)S(1)}) fusion(s32[5625]{0:T(1024)S(1)} %get-tuple-element.11, s32[600]{0:T(1024)} %param.7, s32[5625]{0:T(1024)S(1)} %get-tuple-element.12), kind=kLoop, calls=%fused_computation | loop fusion | flops 20238752 | bytes 92400 | tf_op jit(solution)/shard_map/reduce_max | solution.py:11
  13.2 0.7 add_select_fusion.3
  13.9 1.1 select_reduce_fusion.2
  15.0 0.0 copy-start
  15.0 41.3 %all-gather.2.cloned.1.call-done = bf16[5625,512]{0,1:T(8,128)(2,1)} async-done(((bf16[5625,64]{0,1:T(8,128)(2,1)}), bf16[5625,512]{0,1:T(8,128)(2,1)}) %all-gather.2.cloned.1.call-update) | async-done | bytes 5760016 | tf_op jit(solution)/shard_map/all_gather | solution.py:27
  56.3 6.3 %fusion.4 = f32[288,64,8]{0,2,1:T(8,128)S(1)} fusion(bf16[5625,512]{0,1:T(8,128)(2,1)} %all-gather.2.cloned.1.call-done, bf16[288,5625]{1,0:T(8,128)(2,1)} %param.6, s32[5625]{0:T(1024)S(1)} %xor.15, s32[288]{0:T(512)S(1)} %xor.14), kind=kOutput, calls=%fused_computation.9 | convolution fusion | flops 1662119936 | bytes 9613476 | tf_op jit(solution)/shard_map/dot_general | solution.py:28
  62.6 0.0 copy-done
  62.6 0.6 convolution_bitcast_fusion
  63.3 1.4 copy.20
  64.6 0.0 all-reduce.3.cloned.1.call-update
  64.7 1.3 dynamic-slice
  66.6 159.3 %all-reduce.3.cloned.1.call-done = f32[288,512]{0,1:T(8,128)} async-done(((f32[288,512]{0,1:T(8,128)}), f32[288,512]{0,1:T(8,128)}) %all-reduce.3.cloned.1.call-update) | async-done | bytes 589840
  225.9 1.3 constant_dynamic-slice_fusion
  (3 shorter events, 0.0 us)
Async XLA Ops:
  6.5 49.8 %all-gather.2.cloned.1.call-start = ((), (), s32[]{:S(2)}) async-start(), calls=%async_computation | async-start | bytes 6488064 | tf_op jit(solution)/shard_map/all_gather | solution.py:27
  7.3 218.6 %all-reduce.3.cloned.1.call-start = ((), (), s32[]{:S(2)}) async-start(), calls=%async_computation.1 | async-start | bytes 1572864
  15.0 47.7 %copy-start = (s32[64]{0:T(128)S(1)}, s32[64]{0:T(128)}, u32[]{:S(2)}) copy-start(s32[64]{0:T(128)} %param.9) | copy-start | bytes 772
Sparse Core Ops, SparseCore 0:
  9.5 46.7 all-gather.1
  64.8 161.0 all-reduce.2
where the time goes:
time: 234 us
  waiting for transfers between devices  201 us (86%)
  between operations  14.1 us (6%)
  other arithmetic  7.62 us (3%)
  matrix products  6.95 us (3%)
  local copies, waits for them, and re-layouts  3.95 us (2%)
    unnamed x3, waiting for transfers between devices  160 us
    all_gather x1, waiting for transfers between devices, on_device(): gathered = lax.all_gather(amplitudes, 'grp', axis=1, tiled=True)  41.3 us
    reduce_max x2, other arithmetic, lookup(): jnp.max(jnp.where(indices[:, None] == orbitals[None, :], orbital_irrep[No...  6.88 us
    dot_general x1, matrix products, on_device(): jnp.dot(masked, gathered, preferred_element_type=jnp.float32)  6.33 us
  transfers between devices with their start and end apart: 2, of which 2 were waited for; matrix products, arithmetic and copies ran while one was open for 4% of the time, Pallas kernels for 0%

commit v1 on v0

v1 whole, which is shorter than its diff:
```python
import jax
import jax.numpy as jnp
from jax import lax
from jax.sharding import PartitionSpec as P

V = 600
ROOTS = 8
N_X = 4


def lookup(indices, orbital_irrep):
    orbitals = jnp.arange(orbital_irrep.shape[0], dtype=jnp.int32)
    return jnp.max(
        jnp.where(indices[:, None] == orbitals[None, :], orbital_irrep[None, :], 0), axis=1
    )


def column_symmetry(orbital_irrep, width):
    offset = lax.axis_index("ef") * width
    count = (V - 1 + width) // V + 1
    first = offset // V
    padded = jnp.concatenate([orbital_irrep, jnp.zeros((count,), jnp.int32)])
    outer = lax.dynamic_slice(padded, (first,), (count,))
    table = jnp.bitwise_xor(outer[:, None], orbital_irrep[None, :]).reshape(count * V)
    return lax.dynamic_slice(table, (offset - first * V,), (width,))


def along_x(value, step):
    pairs = [
        (x * 2 + c, (x + step) % N_X * 2 + c) for x in range(N_X) for c in range(2)
    ]
    return lax.ppermute(value, "grp", pairs)


def other_core(value):
    return lax.ppermute(value, "grp", [(g, g ^ 1) for g in range(2 * N_X)])


def product(columns, rows):
    return lax.dot_general(
        columns, rows, (((1,), (1,)), ((), ())), preferred_element_type=jnp.float32
    )


def on_device(amplitudes, ladder, orbital_irrep, panel_rows, slot_pair):
    width = ladder.shape[1]
    rows = ladder.shape[0]
    pairs = slot_pair.shape[0]
    own = amplitudes.T
    half = own.shape[0] // 2
    low, high = own[:half], own[half:]
    left_low = along_x(low, 1)
    right_high = along_x(high, -1)
    left_high = along_x(high, 1)
    right_low = along_x(low, -1)
    far_low = along_x(left_low, 1)
    far_high = along_x(right_high, -1)

    col_sym = column_symmetry(orbital_irrep, width)
    row_sym = jnp.bitwise_xor(
        lookup(panel_rows // V, orbital_irrep), lookup(panel_rows % V, orbital_irrep)
    )
    masked = jnp.where(row_sym[:, None] == col_sym[None, :], ladder, jnp.zeros((), ladder.dtype))
    masked_other = other_core(masked)

    near = [own, left_low, left_high, right_low, right_high]
    far = [far_low, far_high]
    near_other = other_core(jnp.concatenate([product(c, masked_other) for c in near]))
    near_own = [product(c, masked) for c in near]
    far_other = other_core(jnp.concatenate([product(c, masked_other) for c in far]))
    far_own = [product(c, masked) for c in far]
    blocks = jnp.concatenate(near_own + far_own + [near_other, far_other])
    blocks = blocks.reshape(pairs, ROOTS, rows)

    grp = lax.axis_index("grp")
    x, c = grp // 2, grp % 2
    chips = jnp.stack([x, (x + N_X - 1) % N_X, (x + 1) % N_X, (x + 2) % N_X])
    cores = jnp.stack([c, 1 - c])
    groups = (chips[None, :] * 2 + cores[:, None]).reshape(-1)
    held = slot_pair.reshape(2 * N_X, -1)[groups].reshape(-1)
    order = jnp.argmax(held[None, :] == jnp.arange(pairs, dtype=jnp.int32)[:, None], axis=1)
    ordered = jnp.take(blocks, order, axis=0)
    received = lax.all_to_all(ordered, "ef", 0, 0, tiled=True)
    return jnp.sum(received, axis=0).T


def solution(mesh):
    in_specs = (P("ef", "grp"), P("grp", "ef"), P(), P("grp"), P())
    out_specs = P("grp", "ef")
    return jax.shard_map(
        on_device, mesh=mesh, in_specs=in_specs, out_specs=out_specs, check_vma=False
    )
```

time: 234 us -> 120 us (0.51)
  waiting for transfers between devices: 201 us -> 5.63 us
  blocking collectives: 0 us -> 35.6 us
  starting transfers between devices: 0.04 us -> 30 us
  matrix products: 6.95 us -> 33.6 us
  between operations: 14.1 us -> 0.39 us
  local copies, waits for them, and re-layouts: 3.95 us -> 6.39 us
    unnamed x3 -> x0, waiting for transfers between devices: 160 us -> none
    all_gather x1 -> x0, waiting for transfers between devices: 41.3 us -> none  [on_device(): gathered = lax.all_gather(amplitudes, 'grp', axis=1, tiled=True)]
    all_to_all x0 -> x1, blocking collectives: none -> 35.6 us  [on_device(): received = lax.all_to_all(ordered, 'ef', 0, 0, tiled=True)]
    ppermute x0 -> x9, starting transfers between devices: none -> 30 us  [the longest x6 23.8 us: along_x(): return lax.ppermute(value, 'grp', pairs)]
    dot_general x2 -> x14, matrix products: 6.95 us -> 33.6 us  [product(): lax.dot_general(columns, rows, (((1,), (1,)), ((), ())), preferred_elemen...]
    reduce_max x2 -> x1, other arithmetic: 6.88 us -> 1.07 us  [lookup(): jnp.max(jnp.where(indices[:, None] == orbitals[None, :], orbital_irrep[No...]
    ppermute x0 -> x9, waiting for transfers between devices: none -> 5.63 us  [the longest x6 4.75 us: along_x(): return lax.ppermute(value, 'grp', pairs)]
    select_n x1 -> x4, other arithmetic: 0.03 us -> 2.9 us  [the longest x1 2.76 us: on_device(): jnp.where(row_sym[:, None] == col_sym[None, :], ladder, jnp.zeros((), lad...]
  transfers between devices with their start and end apart: 2 -> 9, of which waited for: 2 -> 2; matrix products, arithmetic and copies ran while one was open for 4% -> 22% of each run, Pallas kernels for 0% -> 0%
where the time goes in v1:
time: 120 us; the launch traced here: 119 us
  blocking collectives  35.6 us (30%)
  matrix products  33.6 us (28%)
  starting transfers between devices  30 us (25%)
  other arithmetic  7.02 us (6%)
  local copies, waits for them, and re-layouts  6.39 us (5%)
  waiting for transfers between devices  5.63 us (5%)
    all_to_all x1, blocking collectives, on_device(): received = lax.all_to_all(ordered, 'ef', 0, 0, tiled=True)  35.6 us
    dot_general x14, matrix products, product(): lax.dot_general(columns, rows, (((1,), (1,)), ((), ())), preferred_elemen...  33.6 us
    ppermute x6, starting transfers between devices, along_x(): return lax.ppermute(value, 'grp', pairs)  23.8 us
    ppermute x3, starting transfers between devices, other_core(): return lax.ppermute(value, 'grp', [(g, g ^ 1) for g in range(2 * N_X)])  6.24 us
    ppermute x6, waiting for transfers between devices, along_x(): return lax.ppermute(value, 'grp', pairs)  4.75 us
    select_n x1, other arithmetic, on_device(): jnp.where(row_sym[:, None] == col_sym[None, :], ladder, jnp.zeros((), lad...  2.76 us
  transfers between devices with their start and end apart: 9, of which 2 were waited for; matrix products, arithmetic and copies ran while one was open for 22% of the time, Pallas kernels for 0%

profile of v1, /device:TPU:6, one launch (start us, length us, event | category | flops | bytes accessed | tf_op | source)
XLA Modules:
  0.0 118.6 jit_solution(10333341168007785349)
XLA Ops:
  0.0 2.0 %fusion.14 = (bf16[32,5625]{1,0:T(8,128)(2,1)}, bf16[32,5625]{1,0:T(8,128)(2,1)}) fusion(bf16[64,5625]{1,0:T(8,128)(2,1)} %bitcast.91), kind=kLoop, calls=%fused_computation.55 | loop fusion | bytes 1440000 | tf_op jit(solution)/shard_map/slice | solution.py:51
  2.0 7.7 %collective-permute-start = (bf16[32,5625]{1,0:T(8,128)(2,1)}, bf16[32,5625]{1,0:T(8,128)(2,1)}, u32[]{:S(2)}, u32[]{:S(2)}) collective-permute-start(bf16[32,5625]{1,0:T(8,128)(2,1)} %get-tuple-element.10), channel_id=1, source_target_pairs={{0,128},{64,192},{128,256},{192,320},{256,384},{320,448},{384,0},{... | collective-permute-start | bytes 1080008 | tf_op jit(solution)/shard_map/ppermute | solution.py:32
  9.8 1.9 %collective-permute-start.2 = (bf16[32,5625]{1,0:T(8,128)(2,1)}, bf16[32,5625]{1,0:T(8,128)(2,1)}, u32[]{:S(2)}, u32[]{:S(2)}) collective-permute-start(bf16[32,5625]{1,0:T(8,128)(2,1)} %get-tuple-element.10), channel_id=1, source_target_pairs={{0,384},{64,448},{128,0},{192,64},{256,128},{320,192},{384,256},{4... | collective-permute-start | bytes 1080008 | tf_op jit(solution)/shard_map/ppermute | solution.py:32
  11.7 5.1 %collective-permute-start.1 = (bf16[32,5625]{1,0:T(8,128)(2,1)}, bf16[32,5625]{1,0:T(8,128)(2,1)}, u32[]{:S(2)}, u32[]{:S(2)}) collective-permute-start(bf16[32,5625]{1,0:T(8,128)(2,1)} %get-tuple-element.9), channel_id=1, source_target_pairs={{0,128},{64,192},{128,256},{192,320},{256,384},{320,448},{384,0},{... | collective-permute-start | bytes 1080008 | tf_op jit(solution)/shard_map/ppermute | solution.py:32
  16.8 1.9 %collective-permute-start.3 = (bf16[32,5625]{1,0:T(8,128)(2,1)}, bf16[32,5625]{1,0:T(8,128)(2,1)}, u32[]{:S(2)}, u32[]{:S(2)}) collective-permute-start(bf16[32,5625]{1,0:T(8,128)(2,1)} %get-tuple-element.9), channel_id=1, source_target_pairs={{0,384},{64,448},{128,0},{192,64},{256,128},{320,192},{384,256},{4... | collective-permute-start | bytes 1080008 | tf_op jit(solution)/shard_map/ppermute | solution.py:32
  18.8 0.8 pad_dynamic-slice_fusion
  21.2 1.1 select_reduce_fusion
  22.3 2.8 %compare_select_fusion = bf16[288,5625]{1,0:T(8,128)(2,1)S(1)} fusion(bf16[288,5625]{1,0:T(8,128)(2,1)} %param.6, s32[5625]{0:T(1024)S(1)} %dynamic_slice.7, s32[288]{0:T(512)S(1)} %xor.24), kind=kLoop, calls=%fused_computation.2 | loop fusion | flops 3240000 | bytes 6503652 | tf_op jit(solution)/shard_map/jit(_where)/select_n | solution.py:63
  25.1 1.9 %collective-permute-start.6 = (bf16[288,5625]{1,0:T(8,128)(2,1)S(1)}, bf16[288,5625]{1,0:T(8,128)(2,1)}, u32[]{:S(2)}, u32[]{:S(2)}) collective-permute-start(bf16[288,5625]{1,0:T(8,128)(2,1)S(1)} %compare_select_fusion), channel_id=1, source_target_pairs={{0,64},{64,0},{128,192},{192,128},{256,320},{320,256},{384,448},{4... | collective-permute-start | bytes 9720008 | tf_op jit(solution)/shard_map/ppermute | solution.py:36
  28.8 2.3 %fusion.1 = f32[512,288]{1,0:T(8,128)S(1)} fusion(bf16[288,5625]{1,0:T(8,128)(2,1)S(1)} %compare_select_fusion, bf16[5625,64]{0,1:T(8,128)(2,1)} %param.5), kind=kOutput, calls=%fused_computation.6 | convolution fusion | flops 207360000 | bytes 4058304 | tf_op jit(solution)/shard_map/dot_general | solution.py:40
  31.1 5.1 %collective-permute-start.4 = (bf16[32,5625]{1,0:T(8,128)(2,1)}, bf16[32,5625]{1,0:T(8,128)(2,1)S(1)}, u32[]{:S(2)}, u32[]{:S(2)}) collective-permute-start(bf16[32,5625]{1,0:T(8,128)(2,1)} %collective-permute-done), channel_id=1, source_target_pairs={{0,128},{64,192},{128,256},{192,320},{256,384},{320,448},{384,0},{... | collective-permute-start | bytes 1080008 | tf_op jit(solution)/shard_map/ppermute | solution.py:32
  36.2 2.0 %fusion.11 = f32[512,288]{1,0:T(8,128)S(1)} fusion(f32[512,288]{1,0:T(8,128)S(1)} %fusion.1, bf16[288,5625]{1,0:T(8,128)(2,1)S(1)} %compare_select_fusion, bf16[32,5625]{1,0:T(8,128)(2,1)} %collective-permute-done), kind=kOutput, calls=%fused_computation.28 | convolution fusion | flops 103680000 | bytes 3653184 | tf_op jit(solution)/shard_map/dot_general | solution.py:40
  38.3 1.9 %collective-permute-start.5 = (bf16[32,5625]{1,0:T(8,128)(2,1)}, bf16[32,5625]{1,0:T(8,128)(2,1)S(1)}, u32[]{:S(2)}, u32[]{:S(2)}) collective-permute-start(bf16[32,5625]{1,0:T(8,128)(2,1)} %collective-permute-done.3), channel_id=1, source_target_pairs={{0,384},{64,448},{128,0},{192,64},{256,128},{320,192},{384,256},{4... | collective-permute-start | bytes 1080008 | tf_op jit(solution)/shard_map/ppermute | solution.py:32
  40.2 2.0 %fusion.10 = f32[512,288]{1,0:T(8,128)S(1)} fusion(f32[512,288]{1,0:T(8,128)S(1)} %fusion.11, bf16[288,5625]{1,0:T(8,128)(2,1)S(1)} %compare_select_fusion, bf16[32,5625]{1,0:T(8,128)(2,1)} %collective-permute-done.1), kind=kOutput, calls=%fused_computation.26 | convolution fusion | flops 103680000 | bytes 3653184 | tf_op jit(solution)/shard_map/dot_general | solution.py:40
  42.3 2.0 %fusion.9 = f32[512,288]{1,0:T(8,128)S(1)} fusion(f32[512,288]{1,0:T(8,128)S(1)} %fusion.10, bf16[288,5625]{1,0:T(8,128)(2,1)S(1)} %compare_select_fusion, bf16[32,5625]{1,0:T(8,128)(2,1)} %collective-permute-done.2), kind=kOutput, calls=%fused_computation.24 | convolution fusion | flops 103680000 | bytes 3653184 | tf_op jit(solution)/shard_map/dot_general | solution.py:40
  44.3 2.0 %fusion.8 = f32[512,288]{1,0:T(8,128)S(1)} fusion(f32[512,288]{1,0:T(8,128)S(1)} %fusion.9, bf16[288,5625]{1,0:T(8,128)(2,1)S(1)} %compare_select_fusion, bf16[32,5625]{1,0:T(8,128)(2,1)} %collective-permute-done.3), kind=kOutput, calls=%fused_computation.22 | convolution fusion | flops 103680000 | bytes 3653184 | tf_op jit(solution)/shard_map/dot_general | solution.py:40
  46.4 1.0 fusion.7
  47.4 4.7 %collective-permute-done.5 = bf16[32,5625]{1,0:T(8,128)(2,1)S(1)} collective-permute-done((bf16[32,5625]{1,0:T(8,128)(2,1)}, bf16[32,5625]{1,0:T(8,128)(2,1)S(1)}, u32[]{:S(2)}, u32[]{:S(2)}) %collective-permute-start.5) | collective-permute-done | bytes 360032 | tf_op jit(solution)/shard_map/ppermute | solution.py:32
  52.1 1.0 fusion.6
  53.2 3.1 %fusion = f32[192,288]{1,0:T(8,128)S(1)} fusion(bf16[288,5625]{1,0:T(8,128)(2,1)} %collective-permute-done.6, bf16[5625,64]{0,1:T(8,128)(2,1)S(1)} %copy-done), kind=kOutput, calls=%fused_computation.4 | convolution fusion | flops 207360000 | bytes 4058304 | tf_op jit(solution)/shard_map/dot_general | solution.py:40
  56.3 3.0 %fusion.5 = f32[192,288]{1,0:T(8,128)S(1)} fusion(f32[192,288]{1,0:T(8,128)S(1)} %fusion, bf16[288,5625]{1,0:T(8,128)(2,1)} %collective-permute-done.6, bf16[32,5625]{1,0:T(8,128)(2,1)} %collective-permute-done), kind=kOutput, calls=%fused_computation.16 | convolution fusion | flops 103680000 | bytes 3649152 | tf_op jit(solution)/shard_map/dot_general | solution.py:40
  59.3 3.0 %fusion.4 = f32[192,288]{1,0:T(8,128)S(1)} fusion(f32[192,288]{1,0:T(8,128)S(1)} %fusion.5, bf16[288,5625]{1,0:T(8,128)(2,1)} %collective-permute-done.6, bf16[32,5625]{1,0:T(8,128)(2,1)} %collective-permute-done.1), kind=kOutput, calls=%fused_computation.14 | convolution fusion | flops 103680000 | bytes 3649152 | tf_op jit(solution)/shard_map/dot_general | solution.py:40
  62.3 3.0 %fusion.3 = f32[192,288]{1,0:T(8,128)S(1)} fusion(f32[192,288]{1,0:T(8,128)S(1)} %fusion.4, bf16[288,5625]{1,0:T(8,128)(2,1)} %collective-permute-done.6, bf16[32,5625]{1,0:T(8,128)(2,1)} %collective-permute-done.2), kind=kOutput, calls=%fused_computation.12 | convolution fusion | flops 103680000 | bytes 3649152 | tf_op jit(solution)/shard_map/dot_general | solution.py:40
  65.3 3.0 %fusion.2 = f32[192,288]{1,0:T(8,128)S(1)} fusion(f32[192,288]{1,0:T(8,128)S(1)} %fusion.3, bf16[288,5625]{1,0:T(8,128)(2,1)} %collective-permute-done.6, bf16[32,5625]{1,0:T(8,128)(2,1)} %collective-permute-done.3), kind=kOutput, calls=%fused_computation.10 | convolution fusion | flops 103680000 | bytes 3649152 | tf_op jit(solution)/shard_map/dot_general | solution.py:40
  68.4 1.9 %collective-permute-start.7 = (f32[192,288]{1,0:T(8,128)S(1)}, f32[192,288]{1,0:T(8,128)S(1)}, u32[]{:S(2)}, u32[]{:S(2)}) collective-permute-start(f32[192,288]{1,0:T(8,128)S(1)} %fusion.2), channel_id=1, source_target_pairs={{0,64},{64,0},{128,192},{192,128},{256,320},{320,256},{384,448},{4... | collective-permute-start | bytes 663560 | tf_op jit(solution)/shard_map/ppermute | solution.py:36
  70.3 3.0 %convolution_bitcast_fusion.2 = f32[32,288]{1,0:T(8,128)S(1)} fusion(bf16[288,5625]{1,0:T(8,128)(2,1)} %collective-permute-done.6, bf16[32,5625]{1,0:T(8,128)(2,1)S(1)} %collective-permute-done.5), kind=kOutput, calls=%fused_computation.7 | convolution fusion | flops 103680000 | bytes 3636864 | tf_op jit(solution)/shard_map/dot_general | solution.py:40
  73.3 3.0 %convolution_bitcast_fusion.3 = f32[32,288]{1,0:T(8,128)S(1)} fusion(bf16[288,5625]{1,0:T(8,128)(2,1)} %collective-permute-done.6, bf16[32,5625]{1,0:T(8,128)(2,1)S(1)} %collective-permute-done.4), kind=kOutput, calls=%fused_computation.8 | convolution fusion | flops 103680000 | bytes 3636864 | tf_op jit(solution)/shard_map/dot_general | solution.py:40
  76.3 2.4 %collective-permute-start.8 = (f32[64,288]{1,0:T(8,128)S(1)}, f32[64,288]{1,0:T(8,128)S(1)}, u32[]{:S(2)}, u32[]{:S(2)}) collective-permute-start(f32[64,288]{1,0:T(8,128)S(1)} %pad_maximum_fusion), channel_id=1, source_target_pairs={{0,64},{64,0},{128,192},{192,128},{256,320},{320,256},{384,448},{4... | collective-permute-start | bytes 221192 | tf_op jit(solution)/shard_map/ppermute | solution.py:36
  78.7 0.9 collective-permute-done.8
  79.6 0.9 copy-done.1
  80.5 1.7 %gather_fusion.1 = f32[64,8,288]{2,1,0:T(8,128)S(1)} fusion(f32[64,8,288]{2,1,0:T(8,128)} %bitcast.92, s32[1024]{0:T(1024)S(1)} %pad_clamp_fusion), kind=kCustom, calls=%fused_computation.1 | custom fusion | bytes 1179904 | tf_op jit(solution)/shard_map/jit(_take)/gather | solution.py:82
  82.4 35.6 %all_to_all.5 = f32[64,8,288]{2,1,0:T(8,128)S(1)} all-to-all(f32[64,8,288]{2,1,0:T(8,128)S(1)} %broadcast_select_fusion), channel_id=1, replica_groups=mesh['grp'=8,'ef'=64] {'ef'}, dimensions={0} | all-to-all | bytes 1179648 | tf_op jit(solution)/shard_map/all_to_all | solution.py:83
  (35 shorter events, 4.3 us)
Async XLA Ops:
  2.0 29.1 %collective-permute-start = (bf16[32,5625]{1,0:T(8,128)(2,1)}, bf16[32,5625]{1,0:T(8,128)(2,1)}, u32[]{:S(2)}, u32[]{:S(2)}) collective-permute-start(bf16[32,5625]{1,0:T(8,128)(2,1)} %get-tuple-element.10), channel_id=1, source_target_pairs={{0,128},{64,192},{128,256},{192,320},{256,384},{320,448},{384,0},{... | collective-permute-start | bytes 1080008 | tf_op jit(solution)/shard_map/ppermute | solution.py:32
  9.8 32.5 %collective-permute-start.2 = (bf16[32,5625]{1,0:T(8,128)(2,1)}, bf16[32,5625]{1,0:T(8,128)(2,1)}, u32[]{:S(2)}, u32[]{:S(2)}) collective-permute-start(bf16[32,5625]{1,0:T(8,128)(2,1)} %get-tuple-element.10), channel_id=1, source_target_pairs={{0,384},{64,448},{128,0},{192,64},{256,128},{320,192},{384,256},{4... | collective-permute-start | bytes 1080008 | tf_op jit(solution)/shard_map/ppermute | solution.py:32
  11.7 28.5 %collective-permute-start.1 = (bf16[32,5625]{1,0:T(8,128)(2,1)}, bf16[32,5625]{1,0:T(8,128)(2,1)}, u32[]{:S(2)}, u32[]{:S(2)}) collective-permute-start(bf16[32,5625]{1,0:T(8,128)(2,1)} %get-tuple-element.9), channel_id=1, source_target_pairs={{0,128},{64,192},{128,256},{192,320},{256,384},{320,448},{384,0},{... | collective-permute-start | bytes 1080008 | tf_op jit(solution)/shard_map/ppermute | solution.py:32
  16.8 21.5 %collective-permute-start.3 = (bf16[32,5625]{1,0:T(8,128)(2,1)}, bf16[32,5625]{1,0:T(8,128)(2,1)}, u32[]{:S(2)}, u32[]{:S(2)}) collective-permute-start(bf16[32,5625]{1,0:T(8,128)(2,1)} %get-tuple-element.9), channel_id=1, source_target_pairs={{0,384},{64,448},{128,0},{192,64},{256,128},{320,192},{384,256},{4... | collective-permute-start | bytes 1080008 | tf_op jit(solution)/shard_map/ppermute | solution.py:32
  22.3 4.8 %copy-start.2 = (s32[64]{0:T(128)S(1)}, s32[64]{0:T(128)}, u32[]{:S(2)}) copy-start(s32[64]{0:T(128)} %param.9) | copy-start | bytes 772
  25.1 28.1 %collective-permute-start.6 = (bf16[288,5625]{1,0:T(8,128)(2,1)S(1)}, bf16[288,5625]{1,0:T(8,128)(2,1)}, u32[]{:S(2)}, u32[]{:S(2)}) collective-permute-start(bf16[288,5625]{1,0:T(8,128)(2,1)S(1)} %compare_select_fusion), channel_id=1, source_target_pairs={{0,64},{64,0},{128,192},{192,128},{256,320},{320,256},{384,448},{4... | collective-permute-start | bytes 9720008 | tf_op jit(solution)/shard_map/ppermute | solution.py:36
  31.1 15.3 %collective-permute-start.4 = (bf16[32,5625]{1,0:T(8,128)(2,1)}, bf16[32,5625]{1,0:T(8,128)(2,1)S(1)}, u32[]{:S(2)}, u32[]{:S(2)}) collective-permute-start(bf16[32,5625]{1,0:T(8,128)(2,1)} %collective-permute-done), channel_id=1, source_target_pairs={{0,128},{64,192},{128,256},{192,320},{256,384},{320,448},{384,0},{... | collective-permute-start | bytes 1080008 | tf_op jit(solution)/shard_map/ppermute | solution.py:32
  38.3 13.8 %collective-permute-start.5 = (bf16[32,5625]{1,0:T(8,128)(2,1)}, bf16[32,5625]{1,0:T(8,128)(2,1)S(1)}, u32[]{:S(2)}, u32[]{:S(2)}) collective-permute-start(bf16[32,5625]{1,0:T(8,128)(2,1)} %collective-permute-done.3), channel_id=1, source_target_pairs={{0,384},{64,448},{128,0},{192,64},{256,128},{320,192},{384,256},{4... | collective-permute-start | bytes 1080008 | tf_op jit(solution)/shard_map/ppermute | solution.py:32
  47.4 5.8 %copy-start = (bf16[5625,64]{0,1:T(8,128)(2,1)S(1)}, bf16[5625,64]{0,1:T(8,128)(2,1)}, u32[]{:S(2)}) copy-start(bf16[5625,64]{0,1:T(8,128)(2,1)} %param.5) | copy-start | bytes 2160004
  68.4 10.3 %collective-permute-start.7 = (f32[192,288]{1,0:T(8,128)S(1)}, f32[192,288]{1,0:T(8,128)S(1)}, u32[]{:S(2)}, u32[]{:S(2)}) collective-permute-start(f32[192,288]{1,0:T(8,128)S(1)} %fusion.2), channel_id=1, source_target_pairs={{0,64},{64,0},{128,192},{192,128},{256,320},{320,256},{384,448},{4... | collective-permute-start | bytes 663560 | tf_op jit(solution)/shard_map/ppermute | solution.py:36
  76.3 3.3 %collective-permute-start.8 = (f32[64,288]{1,0:T(8,128)S(1)}, f32[64,288]{1,0:T(8,128)S(1)}, u32[]{:S(2)}, u32[]{:S(2)}) collective-permute-start(f32[64,288]{1,0:T(8,128)S(1)} %pad_maximum_fusion), channel_id=1, source_target_pairs={{0,64},{64,0},{128,192},{192,128},{256,320},{320,256},{384,448},{4... | collective-permute-start | bytes 221192 | tf_op jit(solution)/shard_map/ppermute | solution.py:36
  79.6 0.9 copy-start.1

commit v2 on v0

v2 whole, which is shorter than its diff:
```python
import functools

import jax
import jax.numpy as jnp
from jax import lax
from jax.experimental import pallas as pl
from jax.experimental.pallas import tpu as pltpu
from jax.sharding import PartitionSpec as P

V = 600
ROOTS = 8
N_X = 4
GROUP_SLOTS = 8
CHUNK = 1024
LANES = 128
TAIL = 32
VMEM_LIMIT = 10 << 20

VMEM = pl.BlockSpec(memory_space=pltpu.VMEM)
HBM = pl.BlockSpec(memory_space=pltpu.HBM)
SMEM = pl.BlockSpec(memory_space=pltpu.SMEM)


def lookup(indices, orbital_irrep):
    orbitals = jnp.arange(orbital_irrep.shape[0], dtype=jnp.int32)
    return jnp.max(
        jnp.where(indices[:, None] == orbitals[None, :], orbital_irrep[None, :], 0), axis=1
    )


def column_symmetry(orbital_irrep, width):
    offset = lax.axis_index("ef") * width
    count = (V - 1 + width) // V + 1
    first = offset // V
    padded = jnp.concatenate([orbital_irrep, jnp.zeros((count,), jnp.int32)])
    outer = lax.dynamic_slice(padded, (first,), (count,))
    table = jnp.bitwise_xor(outer[:, None], orbital_irrep[None, :]).reshape(count * V)
    return lax.dynamic_slice(table, (offset - first * V,), (width,))


def neighbour(x, c):
    return (N_X - 1 - x) * c + (x + 1 - 2 * (x % 2)) * (1 - c)


def other_chip(value, link):
    pairs = [(x * 2 + c, neighbour(x, c ^ link) * 2 + c) for x in range(N_X) for c in range(2)]
    return lax.ppermute(value, "grp", pairs)


def other_core(value):
    return lax.ppermute(value, "grp", [(g, g ^ 1) for g in range(2 * N_X)])


def product(columns, rows):
    width = rows.shape[1]
    total = None
    for low in range(0, width, CHUNK):
        span = slice(low, min(low + CHUNK, width))
        left = jnp.concatenate([c[:, span] for c in columns], axis=0)
        part = lax.dot_general(
            left, rows[:, span], (((1,), (1,)), ((), ())), preferred_element_type=jnp.float32
        )
        total = part if total is None else total + part
    return total


def pack(out, pair, source, base):
    block = source[pl.ds(base, ROOTS), :]
    for j in range(ROOTS // 2):
        two = slice(2 * j, 2 * j + 2)
        out[pair, :, j * LANES : (j + 1) * LANES] = block[two, :LANES]
        out[pair, :, (4 + j) * LANES : (5 + j) * LANES] = block[two, LANES : 2 * LANES]
    lane = lax.broadcasted_iota(jnp.int32, (2, LANES), 1)
    tail = block[:2, 2 * LANES :]
    for j in range(1, ROOTS // 2):
        piece = pltpu.roll(block[2 * j : 2 * j + 2, 2 * LANES :], j * TAIL, 1)
        tail = jnp.where(lane >= j * TAIL, piece, tail)
    out[pair, :, 8 * LANES :] = tail


def store_slots(grp, slot_pair, owners, held, out):
    for block, (chip, core) in enumerate(owners):
        group = lax.rem(chip, N_X) * 2 + core
        for slot in range(GROUP_SLOTS):
            pair = slot_pair[group * GROUP_SLOTS + slot]
            pack(out, pair, held, (block * GROUP_SLOTS + slot) * ROOTS)


def owners_of(grp, part):
    x, c = grp[0] // 2, grp[0] % 2
    if part == "chip":
        return (x, c), (x, 1 - c)
    if part == "near":
        a, b = neighbour(x, c), neighbour(x, 1 - c)
        return (a, c), (b, 1 - c), (b, c), (a, 1 - c)
    return (x + 2, c), (x + 2, 1 - c)


def fetching_kernel(part, grp, slot_pair, rows, *refs):
    owners = owners_of(grp, part)
    count = len(owners)
    sources, out = refs[:count], refs[-count - 3]
    *fetched, held, sems = refs[-count - 2 :]
    copies = [
        pltpu.make_async_copy(source, target, sems.at[i])
        for i, (source, target) in enumerate(zip(sources, fetched, strict=True))
    ]
    for copy in copies:
        copy.start()
    for copy in copies:
        copy.wait()
    held[:, : rows.shape[0]] = product(fetched, rows)
    store_slots(grp, slot_pair, owners, held, out)


def far_kernel(grp, slot_pair, rows, far, far_other, near, out, held):
    held[:, : rows.shape[0]] = product((far, far_other), rows)
    store_slots(grp, slot_pair, owners_of(grp, "far"), held, out)


def estimate(columns, rows):
    count = sum(c.shape[0] for c in columns)
    return pl.CostEstimate(
        flops=8 * count * rows.shape[0] * rows.shape[1],
        bytes_accessed=2 * rows.shape[1] * (count + rows.shape[0]),
        transcendentals=0,
    )


def slot_products(part, grp, slot_pair, rows, columns, ordered=None):
    count = sum(c.shape[0] for c in columns)
    held = [pltpu.VMEM((count, 3 * LANES), jnp.float32)]
    if part == "far":
        kernel, place, scratch = far_kernel, VMEM, held
    else:
        kernel, place = functools.partial(fetching_kernel, part), HBM
        scratch = [pltpu.VMEM(c.shape, c.dtype) for c in columns] + held
        scratch.append(pltpu.SemaphoreType.DMA((len(columns),)))
    before = [] if ordered is None else [ordered]
    return pl.pallas_call(
        kernel,
        out_shape=jax.ShapeDtypeStruct((slot_pair.shape[0], 2, 9 * LANES), jnp.float32),
        in_specs=[SMEM, SMEM, VMEM] + [place] * len(columns) + [VMEM] * len(before),
        out_specs=VMEM,
        scratch_shapes=scratch,
        input_output_aliases={3 + len(columns): 0} if before else {},
        compiler_params=pltpu.CompilerParams(vmem_limit_bytes=VMEM_LIMIT),
        cost_estimate=estimate(columns, rows),
    )(grp, slot_pair, rows, *columns, *before)


def total_kernel(received, out):
    total = jnp.sum(received[...], axis=0)
    for j in range(ROOTS // 2):
        two = slice(2 * j, 2 * j + 2)
        out[two, :LANES] = total[:, j * LANES : (j + 1) * LANES]
        out[two, LANES : 2 * LANES] = total[:, (4 + j) * LANES : (5 + j) * LANES]
        tail = total[:, 8 * LANES :]
        tail = tail if j == 0 else pltpu.roll(tail, LANES - j * TAIL, 1)
        out[two, 2 * LANES :] = tail[:, :TAIL]


def add_received(received, rows):
    return pl.pallas_call(
        total_kernel,
        out_shape=jax.ShapeDtypeStruct((ROOTS, rows), jnp.float32),
        in_specs=[VMEM],
        out_specs=VMEM,
        compiler_params=pltpu.CompilerParams(vmem_limit_bytes=VMEM_LIMIT),
    )(received)


def on_device(amplitudes, ladder, orbital_irrep, panel_rows, slot_pair):
    grp = lax.axis_index("grp").astype(jnp.int32).reshape(1)
    own = amplitudes.T
    mine = other_chip(own, 0)

    col_sym = column_symmetry(orbital_irrep, ladder.shape[1])
    row_sym = jnp.bitwise_xor(
        lookup(panel_rows // V, orbital_irrep), lookup(panel_rows % V, orbital_irrep)
    )
    masked = jnp.where(row_sym[:, None] == col_sym[None, :], ladder, jnp.zeros((), ladder.dtype))
    later, masked = lax.optimization_barrier((own, masked))
    theirs = other_chip(later, 1)

    own_other = other_core(own)
    ordered = slot_products("chip", grp, slot_pair, masked, (own, own_other))
    mine, ordered = lax.optimization_barrier((mine, ordered))
    far = other_chip(mine, 1)
    mine_late, theirs = lax.optimization_barrier((mine, theirs))
    mine_other, theirs_other = other_core(mine_late), other_core(theirs)
    near = (mine, mine_other, theirs, theirs_other)
    ordered = slot_products("near", grp, slot_pair, masked, near, ordered)
    far_other = other_core(far)
    ordered = slot_products("far", grp, slot_pair, masked, (far, far_other), ordered)
    received = lax.all_to_all(ordered, "ef", 0, 0, tiled=True)
    return add_received(received, ladder.shape[0]).T


def solution(mesh):
    in_specs = (P("ef", "grp"), P("grp", "ef"), P(), P("grp"), P())
    out_specs = P("grp", "ef")
    return jax.shard_map(
        on_device, mesh=mesh, in_specs=in_specs, out_specs=out_specs, check_vma=False
    )
```

time: 234 us -> 80.8 us (0.35)
  the two profiles are of different devices: /device:TPU:6 before, /device:TPU:8 now
where the time goes in v2:
time: 80.8 us; the launch traced here: 80.3 us
  blocking collectives  37.6 us (47%)
  starting transfers between devices  18.6 us (23%)
  Pallas kernels  10.1 us (12%)
  waiting for transfers between devices  7.52 us (9%)
  other arithmetic  5.28 us (7%)
  local copies, waits for them, and re-layouts  0.95 us (1%)
    all_to_all x1, blocking collectives, on_device(): received = lax.all_to_all(ordered, 'ef', 0, 0, tiled=True)  37.6 us
    ppermute x3, starting transfers between devices, other_chip(): return lax.ppermute(value, 'grp', pairs)  10.5 us
    pallas_call x3, Pallas kernels, slot_products(): pl.pallas_call(kernel, out_shape=jax.ShapeDtypeStruct((slot_pair.shape[0]...  9.2 us
    ppermute x4, starting transfers between devices, other_core(): return lax.ppermute(value, 'grp', [(g, g ^ 1) for g in range(2 * N_X)])  8.13 us
    ppermute x3, waiting for transfers between devices, other_chip(): return lax.ppermute(value, 'grp', pairs)  7.51 us
    select_n x1, other arithmetic, on_device(): jnp.where(row_sym[:, None] == col_sym[None, :], ladder, jnp.zeros((), lad...  2.76 us
  transfers between devices with their start and end apart: 7, of which 2 were waited for; matrix products, arithmetic and copies ran while one was open for 8% of the time, Pallas kernels for 9%

profile of v2, /device:TPU:8, one launch (start us, length us, event | category | flops | bytes accessed | tf_op | source)
XLA Modules:
  0.0 80.3 jit_solution(8067292240744002375)
XLA Ops:
  0.0 1.9 %collective-permute-start.1 = (bf16[64,5625]{1,0:T(8,128)(2,1)}, bf16[64,5625]{1,0:T(8,128)(2,1)}, u32[]{:S(2)}, u32[]{:S(2)}) collective-permute-start(bf16[64,5625]{1,0:T(8,128)(2,1)} %bitcast.1.refs_0_), channel_id=1, source_target_pairs={{0,64},{64,0},{128,192},{192,128},{256,320},{320,256},{384,448},{4... | collective-permute-start | bytes 2160008 | tf_op jit(solution)/shard_map/ppermute | solution.py:51
  1.9 3.4 %collective-permute-start = (bf16[64,5625]{1,0:T(8,128)(2,1)}, bf16[64,5625]{1,0:T(8,128)(2,1)}, u32[]{:S(2)}, u32[]{:S(2)}) collective-permute-start(bf16[64,5625]{1,0:T(8,128)(2,1)} %bitcast.1.refs_0_), channel_id=1, source_target_pairs={{0,128},{64,448},{128,0},{192,320},{256,384},{320,192},{384,256},{... | collective-permute-start | bytes 2160008 | tf_op jit(solution)/shard_map/ppermute | solution.py:47
  5.4 0.8 pad_dynamic-slice_fusion
  6.1 0.8 broadcast_xor_fusion
  6.9 0.1 xor.28
  7.0 0.7 add_select_fusion.1
  7.7 0.1 dynamic_slice.7
  7.8 1.1 %select_reduce_fusion = (s32[288]{0:T(512)S(1)}, s32[288]{0:T(512)S(1)}) fusion(s32[288]{0:T(512)S(1)} %get-tuple-element.20, s32[600]{0:T(1024)} %param.7, s32[288]{0:T(512)S(1)} %get-tuple-element.19), kind=kLoop, calls=%fused_computation.1 | loop fusion | flops 1036224 | bytes 7008 | tf_op jit(solution)/shard_map/reduce_max | solution.py:26
  8.9 0.0 copy-start
  8.9 2.8 %compare_select_fusion.rows = bf16[288,5625]{1,0:T(8,128)(2,1)S(1)} fusion(bf16[288,5625]{1,0:T(8,128)(2,1)} %param.6, s32[5625]{0:T(1024)S(1)} %dynamic_slice.7, s32[288]{0:T(512)S(1)} %xor.24), kind=kLoop, calls=%fused_computation | loop fusion | flops 3240000 | bytes 6503652 | tf_op jit(solution)/shard_map/jit(_where)/select_n | solution.py:182
  11.6 4.0 %collective-permute-start.4 = (bf16[64,5625]{1,0:T(8,128)(2,1)}, bf16[64,5625]{1,0:T(8,128)(2,1)}, u32[]{:S(2)}, u32[]{:S(2)}) collective-permute-start(bf16[64,5625]{1,0:T(8,128)(2,1)} %bitcast.1.refs_0_), channel_id=1, source_target_pairs={{0,384},{64,192},{128,256},{192,64},{256,128},{320,448},{384,0},{4... | collective-permute-start | bytes 2160008 | tf_op jit(solution)/shard_map/ppermute | solution.py:47
  15.6 0.0 collective-permute-done.1.refs_1_
  15.7 0.0 copy-done
  15.7 3.4 %shard_map.55.refs_4_ = f32[64,2,1152]{2,1,0:T(2,128)S(1)} custom-call(s32[1]{0:T(128)} %bitcast.grp, s32[64]{0:T(128)S(1)} %copy-done, bf16[288,5625]{1,0:T(8,128)(2,1)S(1)} %compare_select_fusion.rows, bf16[64,5625]{1,0:T(8,128)(2,1)} %bitcast.1.refs_0_, bf16[64,5625]{1,0:T(8,128)(2,1)} %collective-permute-done.1.refs_1_), custom_call_target="tpu_custom_call" | custom-call | flops 1658880000 | bytes 4680000 | tf_op jit(solution)/shard_map/pallas_call | solution.py:140
  19.1 0.0 collective-permute-done.refs_0_
  19.1 3.0 %collective-permute-start.2 = (bf16[64,5625]{1,0:T(8,128)(2,1)}, bf16[64,5625]{1,0:T(8,128)(2,1)S(1)}, u32[]{:S(2)}, u32[]{:S(2)}) collective-permute-start(bf16[64,5625]{1,0:T(8,128)(2,1)} %collective-permute-done.refs_0_), channel_id=1, source_target_pairs={{0,384},{64,192},{128,256},{192,64},{256,128},{320,448},{384,0},{4... | collective-permute-start | bytes 2160008 | tf_op jit(solution)/shard_map/ppermute | solution.py:47
  22.1 4.2 %collective-permute-done.4.refs_2_ = bf16[64,5625]{1,0:T(8,128)(2,1)} collective-permute-done((bf16[64,5625]{1,0:T(8,128)(2,1)}, bf16[64,5625]{1,0:T(8,128)(2,1)}, u32[]{:S(2)}, u32[]{:S(2)}) %collective-permute-start.4) | collective-permute-done | bytes 720032 | tf_op jit(solution)/shard_map/ppermute | solution.py:47
  26.3 1.9 %collective-permute-start.5 = (bf16[64,5625]{1,0:T(8,128)(2,1)}, bf16[64,5625]{1,0:T(8,128)(2,1)S(1)}, u32[]{:S(2)}, u32[]{:S(2)}) collective-permute-start(bf16[64,5625]{1,0:T(8,128)(2,1)} %collective-permute-done.refs_0_), channel_id=1, source_target_pairs={{0,64},{64,0},{128,192},{192,128},{256,320},{320,256},{384,448},{4... | collective-permute-start | bytes 2160008 | tf_op jit(solution)/shard_map/ppermute | solution.py:51
  28.3 2.4 %collective-permute-start.6 = (bf16[64,5625]{1,0:T(8,128)(2,1)}, bf16[64,5625]{1,0:T(8,128)(2,1)S(1)}, u32[]{:S(2)}, u32[]{:S(2)}) collective-permute-start(bf16[64,5625]{1,0:T(8,128)(2,1)} %collective-permute-done.4.refs_2_), channel_id=1, source_target_pairs={{0,64},{64,0},{128,192},{192,128},{256,320},{320,256},{384,448},{4... | collective-permute-start | bytes 2160008 | tf_op jit(solution)/shard_map/ppermute | solution.py:51
  30.7 3.3 %collective-permute-done.2.far = bf16[64,5625]{1,0:T(8,128)(2,1)S(1)} collective-permute-done((bf16[64,5625]{1,0:T(8,128)(2,1)}, bf16[64,5625]{1,0:T(8,128)(2,1)S(1)}, u32[]{:S(2)}, u32[]{:S(2)}) %collective-permute-start.2) | collective-permute-done | bytes 720032 | tf_op jit(solution)/shard_map/ppermute | solution.py:47
  34.0 1.9 %collective-permute-start.3 = (bf16[64,5625]{1,0:T(8,128)(2,1)S(1)}, bf16[64,5625]{1,0:T(8,128)(2,1)S(1)}, u32[]{:S(2)}, u32[]{:S(2)}) collective-permute-start(bf16[64,5625]{1,0:T(8,128)(2,1)S(1)} %collective-permute-done.2.far), channel_id=1, source_target_pairs={{0,64},{64,0},{128,192},{192,128},{256,320},{320,256},{384,448},{4... | collective-permute-start | bytes 2160008 | tf_op jit(solution)/shard_map/ppermute | solution.py:51
  35.9 0.0 collective-permute-done.5.refs_1_
  35.9 0.0 collective-permute-done.6.refs_3_
  35.9 3.8 %shard_map.56.near = f32[64,2,1152]{2,1,0:T(2,128)S(1)} custom-call(s32[1]{0:T(128)} %bitcast.grp, s32[64]{0:T(128)S(1)} %copy-done, bf16[288,5625]{1,0:T(8,128)(2,1)S(1)} %compare_select_fusion.rows, bf16[64,5625]{1,0:T(8,128)(2,1)} %collective-permute-done.refs_0_, ...), custom_call_target="tpu_custom_call", output_to_operand_aliasing={{}: (7, {})} | custom-call | flops 3317760000 | bytes 6120000 | tf_op jit(solution)/shard_map/pallas_call | solution.py:140
  39.7 0.0 collective-permute-done.3.far_other
  39.7 2.0 %shard_map.57 = f32[64,2,1152]{2,1,0:T(2,128)S(1)} custom-call(s32[1]{0:T(128)} %bitcast.grp, s32[64]{0:T(128)S(1)} %copy-done, bf16[288,5625]{1,0:T(8,128)(2,1)S(1)} %compare_select_fusion.rows, bf16[64,5625]{1,0:T(8,128)(2,1)S(1)} %collective-permute-done.2.far, ...), custom_call_target="tpu_custom_call", output_to_operand_aliasing={{}: (5, {})} | custom-call | flops 1658880000 | bytes 4680000 | tf_op jit(solution)/shard_map/pallas_call | solution.py:140
  41.7 37.6 %all_to_all.5.received = f32[64,2,1152]{2,1,0:T(2,128)S(1)} all-to-all(f32[64,2,1152]{2,1,0:T(2,128)S(1)} %shard_map.57), channel_id=1, replica_groups=mesh['grp'=8,'ef'=64] {'ef'}, dimensions={0} | all-to-all | bytes 1179648 | tf_op jit(solution)/shard_map/all_to_all | solution.py:196
  79.4 0.9 %shard_map.58 = f32[8,288]{1,0:T(8,128)} custom-call(f32[64,2,1152]{2,1,0:T(2,128)S(1)} %all_to_all.5.received), custom_call_target="tpu_custom_call" | custom-call | tf_op jit(solution)/shard_map/pallas_call | solution.py:164
  (1 shorter events, 0.0 us)
Async XLA Ops:
  0.0 15.7 %collective-permute-start.1 = (bf16[64,5625]{1,0:T(8,128)(2,1)}, bf16[64,5625]{1,0:T(8,128)(2,1)}, u32[]{:S(2)}, u32[]{:S(2)}) collective-permute-start(bf16[64,5625]{1,0:T(8,128)(2,1)} %bitcast.1.refs_0_), channel_id=1, source_target_pairs={{0,64},{64,0},{128,192},{192,128},{256,320},{320,256},{384,448},{4... | collective-permute-start | bytes 2160008 | tf_op jit(solution)/shard_map/ppermute | solution.py:51
  1.9 17.1 %collective-permute-start = (bf16[64,5625]{1,0:T(8,128)(2,1)}, bf16[64,5625]{1,0:T(8,128)(2,1)}, u32[]{:S(2)}, u32[]{:S(2)}) collective-permute-start(bf16[64,5625]{1,0:T(8,128)(2,1)} %bitcast.1.refs_0_), channel_id=1, source_target_pairs={{0,128},{64,448},{128,0},{192,320},{256,384},{320,192},{384,256},{... | collective-permute-start | bytes 2160008 | tf_op jit(solution)/shard_map/ppermute | solution.py:47
  8.9 6.8 %copy-start = (s32[64]{0:T(128)S(1)}, s32[64]{0:T(128)}, u32[]{:S(2)}) copy-start(s32[64]{0:T(128)} %slot_pair.5) | copy-start | bytes 772
  11.6 14.7 %collective-permute-start.4 = (bf16[64,5625]{1,0:T(8,128)(2,1)}, bf16[64,5625]{1,0:T(8,128)(2,1)}, u32[]{:S(2)}, u32[]{:S(2)}) collective-permute-start(bf16[64,5625]{1,0:T(8,128)(2,1)} %bitcast.1.refs_0_), channel_id=1, source_target_pairs={{0,384},{64,192},{128,256},{192,64},{256,128},{320,448},{384,0},{4... | collective-permute-start | bytes 2160008 | tf_op jit(solution)/shard_map/ppermute | solution.py:47
  19.1 14.9 %collective-permute-start.2 = (bf16[64,5625]{1,0:T(8,128)(2,1)}, bf16[64,5625]{1,0:T(8,128)(2,1)S(1)}, u32[]{:S(2)}, u32[]{:S(2)}) collective-permute-start(bf16[64,5625]{1,0:T(8,128)(2,1)} %collective-permute-done.refs_0_), channel_id=1, source_target_pairs={{0,384},{64,192},{128,256},{192,64},{256,128},{320,448},{384,0},{4... | collective-permute-start | bytes 2160008 | tf_op jit(solution)/shard_map/ppermute | solution.py:47
  26.3 9.5 %collective-permute-start.5 = (bf16[64,5625]{1,0:T(8,128)(2,1)}, bf16[64,5625]{1,0:T(8,128)(2,1)S(1)}, u32[]{:S(2)}, u32[]{:S(2)}) collective-permute-start(bf16[64,5625]{1,0:T(8,128)(2,1)} %collective-permute-done.refs_0_), channel_id=1, source_target_pairs={{0,64},{64,0},{128,192},{192,128},{256,320},{320,256},{384,448},{4... | collective-permute-start | bytes 2160008 | tf_op jit(solution)/shard_map/ppermute | solution.py:51
  28.3 7.6 %collective-permute-start.6 = (bf16[64,5625]{1,0:T(8,128)(2,1)}, bf16[64,5625]{1,0:T(8,128)(2,1)S(1)}, u32[]{:S(2)}, u32[]{:S(2)}) collective-permute-start(bf16[64,5625]{1,0:T(8,128)(2,1)} %collective-permute-done.4.refs_2_), channel_id=1, source_target_pairs={{0,64},{64,0},{128,192},{192,128},{256,320},{320,256},{384,448},{4... | collective-permute-start | bytes 2160008 | tf_op jit(solution)/shard_map/ppermute | solution.py:51
  34.0 5.8 %collective-permute-start.3 = (bf16[64,5625]{1,0:T(8,128)(2,1)S(1)}, bf16[64,5625]{1,0:T(8,128)(2,1)S(1)}, u32[]{:S(2)}, u32[]{:S(2)}) collective-permute-start(bf16[64,5625]{1,0:T(8,128)(2,1)S(1)} %collective-permute-done.2.far), channel_id=1, source_target_pairs={{0,64},{64,0},{128,192},{192,128},{256,320},{320,256},{384,448},{4... | collective-permute-start | bytes 2160008 | tf_op jit(solution)/shard_map/ppermute | solution.py:51

commit v3 on v2

v3 whole, which is shorter than its diff:
```python
import functools

import jax
import jax.numpy as jnp
from jax import lax
from jax.experimental import pallas as pl
from jax.experimental.pallas import tpu as pltpu
from jax.sharding import PartitionSpec as P

V = 600
ROOTS = 8
N_X = 4
GROUP_SLOTS = 8
CHUNK = 1024
LANES = 128
TAIL = 32
STEPS = 32000.0
SMALLEST = 1e-30
VMEM_LIMIT = 10 << 20

VMEM = pl.BlockSpec(memory_space=pltpu.VMEM)
SMEM = pl.BlockSpec(memory_space=pltpu.SMEM)


def lookup(indices, orbital_irrep):
    orbitals = jnp.arange(orbital_irrep.shape[0], dtype=jnp.int32)
    return jnp.max(
        jnp.where(indices[:, None] == orbitals[None, :], orbital_irrep[None, :], 0), axis=1
    )


def column_symmetry(orbital_irrep, width):
    offset = lax.axis_index("ef") * width
    count = (V - 1 + width) // V + 1
    first = offset // V
    padded = jnp.concatenate([orbital_irrep, jnp.zeros((count,), jnp.int32)])
    outer = lax.dynamic_slice(padded, (first,), (count,))
    table = jnp.bitwise_xor(outer[:, None], orbital_irrep[None, :]).reshape(count * V)
    return lax.dynamic_slice(table, (offset - first * V,), (width,))


def neighbour(x, c):
    return (N_X - 1 - x) * c + (x + 1 - 2 * (x % 2)) * (1 - c)


def other_chip(value, link):
    pairs = [(x * 2 + c, neighbour(x, c ^ link) * 2 + c) for x in range(N_X) for c in range(2)]
    return lax.ppermute(value, "grp", pairs)


def other_core(value):
    return lax.ppermute(value, "grp", [(g, g ^ 1) for g in range(2 * N_X)])


def product(columns, rows):
    width = rows.shape[1]
    total = None
    for low in range(0, width, CHUNK):
        span = slice(low, min(low + CHUNK, width))
        left = jnp.concatenate([c[:, span] for c in columns], axis=0)
        part = lax.dot_general(
            left, rows[:, span], (((1,), (1,)), ((), ())), preferred_element_type=jnp.float32
        )
        total = part if total is None else total + part
    return total


def pack(out, pair, block, exponent):
    for j in range(ROOTS // 2):
        two = slice(2 * j, 2 * j + 2)
        out[pair, :, j * LANES : (j + 1) * LANES] = block[two, :LANES]
        out[pair, :, (4 + j) * LANES : (5 + j) * LANES] = block[two, LANES : 2 * LANES]
    lane = lax.broadcasted_iota(jnp.int32, (2, LANES), 1)
    tail = block[:2, 2 * LANES :]
    for j in range(1, ROOTS // 2):
        piece = pltpu.roll(block[2 * j : 2 * j + 2, 2 * LANES :], j * TAIL, 1)
        tail = jnp.where(lane >= j * TAIL, piece, tail)
    out[pair, :, 8 * LANES : 9 * LANES] = tail
    out[pair, :, 9 * LANES :] = exponent


def store_slots(grp, slot_pair, owners, held, steps, exponents, out):
    count = held.shape[0] // ROOTS
    values = held[...].reshape(count, ROOTS, held.shape[1])
    largest = jnp.max(jnp.max(jnp.abs(values), axis=1, keepdims=True), axis=2, keepdims=True)
    exponent = jnp.floor(jnp.log2(jnp.maximum(largest, SMALLEST))) + 1.0
    scale = jnp.exp2(-exponent) * STEPS
    steps[...] = jnp.round(values * scale).astype(jnp.int32)
    exponents[...] = jnp.broadcast_to(exponent, exponents.shape).astype(jnp.int32)
    for block, (chip, core) in enumerate(owners):
        group = lax.rem(chip, N_X) * 2 + core
        for slot in range(GROUP_SLOTS):
            pair = slot_pair[group * GROUP_SLOTS + slot]
            index = block * GROUP_SLOTS + slot
            pack(out, pair, steps[index], exponents[index])


def owners_of(grp, part):
    x, c = grp[0] // 2, grp[0] % 2
    a, b = neighbour(x, c), neighbour(x, 1 - c)
    if part == "first":
        return (x, c), (x, 1 - c), (a, c)
    if part == "second":
        return (b, c), (b, 1 - c), (a, 1 - c)
    return (x + 2, c), (x + 2, 1 - c)


def product_kernel(part, grp, slot_pair, rows, *refs):
    owners = owners_of(grp, part)
    out, held, steps, exponents = refs[-4:]
    count = rows.shape[0]
    held[:, 2 * LANES :] = jnp.zeros((held.shape[0], LANES), held.dtype)
    held[:, :count] = product(refs[: len(owners)], rows)
    store_slots(grp, slot_pair, owners, held, steps, exponents, out)


def estimate(columns, rows):
    count = sum(c.shape[0] for c in columns)
    return pl.CostEstimate(
        flops=8 * count * rows.shape[0] * rows.shape[1],
        bytes_accessed=2 * rows.shape[1] * (count + rows.shape[0]),
        transcendentals=0,
    )


def slot_products(part, grp, slot_pair, rows, columns, ordered=None):
    count = sum(c.shape[0] for c in columns)
    before = [] if ordered is None else [ordered]
    return pl.pallas_call(
        functools.partial(product_kernel, part),
        out_shape=jax.ShapeDtypeStruct((slot_pair.shape[0], 2, 10 * LANES), jnp.int32),
        in_specs=[SMEM, SMEM, VMEM] + [VMEM] * len(columns) + [VMEM] * len(before),
        out_specs=VMEM,
        scratch_shapes=[
            pltpu.VMEM((count, 3 * LANES), jnp.float32),
            pltpu.VMEM((count // ROOTS, ROOTS, 3 * LANES), jnp.int32),
            pltpu.VMEM((count // ROOTS, 2, LANES), jnp.int32),
        ],
        input_output_aliases={3 + len(columns): 0} if before else {},
        compiler_params=pltpu.CompilerParams(vmem_limit_bytes=VMEM_LIMIT),
        cost_estimate=estimate(columns, rows),
    )(grp, slot_pair, rows, *columns, *before)


def total_kernel(received, out):
    width = 9 * LANES
    unit = jnp.exp2(received[:, :, width:].astype(jnp.float32)) * (1.0 / STEPS)
    for j in range(9):
        steps = received[:, :, j * LANES : (j + 1) * LANES].astype(jnp.float32)
        total = jnp.sum(steps * unit, axis=0)
        if j < 8:
            row = 2 * (j % 4)
            out[row : row + 2, j // 4 * LANES : (j // 4 + 1) * LANES] = total
        else:
            for i in range(ROOTS // 2):
                tail = total if i == 0 else pltpu.roll(total, LANES - i * TAIL, 1)
                out[2 * i : 2 * i + 2, 2 * LANES :] = tail[:, :TAIL]


def add_received(received, rows):
    return pl.pallas_call(
        total_kernel,
        out_shape=jax.ShapeDtypeStruct((ROOTS, rows), jnp.float32),
        in_specs=[VMEM],
        out_specs=VMEM,
        compiler_params=pltpu.CompilerParams(vmem_limit_bytes=VMEM_LIMIT),
    )(received)


def on_device(amplitudes, ladder, orbital_irrep, panel_rows, slot_pair):
    grp = lax.axis_index("grp").astype(jnp.int32).reshape(1)
    own = amplitudes.T
    mine = other_chip(own, 0)

    col_sym = column_symmetry(orbital_irrep, ladder.shape[1])
    row_sym = jnp.bitwise_xor(
        lookup(panel_rows // V, orbital_irrep), lookup(panel_rows % V, orbital_irrep)
    )
    first, row_sym, col_sym = lax.optimization_barrier((own, row_sym, col_sym))
    theirs, own_other = other_chip(first, 1), other_core(first)
    mine, row_sym, col_sym = lax.optimization_barrier((mine, row_sym, col_sym))
    far = other_chip(mine, 1)
    masked = jnp.where(row_sym[:, None] == col_sym[None, :], ladder, jnp.zeros((), ladder.dtype))
    ordered = slot_products("first", grp, slot_pair, masked, (own, own_other, mine))
    mine, theirs, ordered = lax.optimization_barrier((mine, theirs, ordered))
    mine_other, theirs_other = other_core(mine), other_core(theirs)
    near = (theirs, mine_other, theirs_other)
    ordered = slot_products("second", grp, slot_pair, masked, near, ordered)
    far_other = other_core(far)
    ordered = slot_products("far", grp, slot_pair, masked, (far, far_other), ordered)
    received = lax.all_to_all(ordered.astype(jnp.int16), "ef", 0, 0, tiled=True)
    return add_received(received.astype(jnp.int32), ladder.shape[0]).T


def solution(mesh):
    in_specs = (P("ef", "grp"), P("grp", "ef"), P(), P("grp"), P())
    out_specs = P("grp", "ef")
    return jax.shard_map(
        on_device, mesh=mesh, in_specs=in_specs, out_specs=out_specs, check_vma=False
    )
```

time: 80.8 us -> 73.1 us (0.905)
  the two profiles are of different devices: /device:TPU:8 before, /device:TPU:6 now
where the time goes in v3:
time: 73.1 us; the launch traced here: 71.7 us
  blocking collectives  31.2 us (43%)
  starting transfers between devices  24.2 us (33%)
  Pallas kernels  8 us (11%)
  other arithmetic  5.81 us (8%)
  waiting for transfers between devices  1.22 us (2%)
  local copies, waits for them, and re-layouts  0.95 us (1%)
    all_to_all x1, blocking collectives, on_device(): received = lax.all_to_all(ordered.astype(jnp.int16), 'ef', 0, 0, tiled=True)  31.2 us
    ppermute x3, starting transfers between devices, other_chip(): return lax.ppermute(value, 'grp', pairs)  16.1 us
    ppermute x4, starting transfers between devices, other_core(): return lax.ppermute(value, 'grp', [(g, g ^ 1) for g in range(2 * N_X)])  8.16 us
    pallas_call x3, Pallas kernels, slot_products(): pl.pallas_call(functools.partial(product_kernel, part), out_shape=jax.Sha...  6.97 us
    select_n x1, other arithmetic, on_device(): jnp.where(row_sym[:, None] == col_sym[None, :], ladder, jnp.zeros((), lad...  2.72 us
  transfers between devices with their start and end apart: 7, of which 1 were waited for; matrix products, arithmetic and copies ran while one was open for 9% of the time, Pallas kernels for 7%

profile of v3, /device:TPU:6, one launch (start us, length us, event | category | flops | bytes accessed | tf_op | source)
XLA Modules:
  0.0 71.7 jit_solution(3806290149469597632)
XLA Ops:
  0.0 2.7 %collective-permute-start = (bf16[64,5625]{1,0:T(8,128)(2,1)}, bf16[64,5625]{1,0:T(8,128)(2,1)S(1)}, u32[]{:S(2)}, u32[]{:S(2)}) collective-permute-start(bf16[64,5625]{1,0:T(8,128)(2,1)} %bitcast.3), channel_id=1, source_target_pairs={{0,128},{64,448},{128,0},{192,320},{256,384},{320,192},{384,256},{... | collective-permute-start | bytes 2160008 | tf_op jit(solution)/shard_map/ppermute | solution.py:48
  2.8 0.8 %pad_dynamic-slice_fusion = s32[11]{0:T(128)S(1)} fusion(s32[]{:T(128)S(6)} %select_n.38, s32[600]{0:T(1024)} %param.7), kind=kLoop, calls=%fused_computation.6 | loop fusion | bytes 2448 | tf_op jit(solution)/shard_map/dynamic_slice | solution.py:37
  3.5 0.8 %broadcast_xor_fusion = s32[11,600]{1,0:T(8,128)S(1)} fusion(s32[600]{0:T(1024)} %param.7, s32[11]{0:T(128)S(1)} %pad_dynamic-slice_fusion), kind=kLoop, calls=%fused_computation.5 | loop fusion | flops 6600 | bytes 28844 | tf_op jit(solution)/shard_map/xor | solution.py:38
  4.3 0.1 xor.24
  4.4 0.1 dynamic_slice.7
  4.5 0.7 add_select_fusion.1
  5.2 1.1 %select_reduce_fusion = (s32[288]{0:T(512)S(1)}, s32[288]{0:T(512)S(1)}) fusion(s32[288]{0:T(512)S(1)} %get-tuple-element.26, s32[600]{0:T(1024)} %param.7, s32[288]{0:T(512)S(1)} %get-tuple-element.25), kind=kLoop, calls=%fused_computation.1 | loop fusion | flops 1036224 | bytes 7008 | tf_op jit(solution)/shard_map/reduce_max | solution.py:27
  6.3 1.9 %collective-permute-start.4 = (bf16[64,5625]{1,0:T(8,128)(2,1)}, bf16[64,5625]{1,0:T(8,128)(2,1)S(1)}, u32[]{:S(2)}, u32[]{:S(2)}) collective-permute-start(bf16[64,5625]{1,0:T(8,128)(2,1)} %bitcast.4), channel_id=1, source_target_pairs={{0,64},{64,0},{128,192},{192,128},{256,320},{320,256},{384,448},{4... | collective-permute-start | bytes 2160008 | tf_op jit(solution)/shard_map/ppermute | solution.py:52
  8.2 6.9 %collective-permute-start.3 = (bf16[64,5625]{1,0:T(8,128)(2,1)}, bf16[64,5625]{1,0:T(8,128)(2,1)S(1)}, u32[]{:S(2)}, u32[]{:S(2)}) collective-permute-start(bf16[64,5625]{1,0:T(8,128)(2,1)} %bitcast.5), channel_id=1, source_target_pairs={{0,384},{64,192},{128,256},{192,64},{256,128},{320,448},{384,0},{4... | collective-permute-start | bytes 2160008 | tf_op jit(solution)/shard_map/ppermute | solution.py:48
  15.1 0.0 copy-start
  15.2 0.0 copy-start.1
  15.2 0.0 collective-permute-done.refs_2_
  15.2 6.4 %collective-permute-start.1 = (bf16[64,5625]{1,0:T(8,128)(2,1)S(1)}, bf16[64,5625]{1,0:T(8,128)(2,1)S(1)}, u32[]{:S(2)}, u32[]{:S(2)}) collective-permute-start(bf16[64,5625]{1,0:T(8,128)(2,1)S(1)} %collective-permute-done.refs_2_), channel_id=1, source_target_pairs={{0,384},{64,192},{128,256},{192,64},{256,128},{320,448},{384,0},{4... | collective-permute-start | bytes 2160008 | tf_op jit(solution)/shard_map/ppermute | solution.py:48
  21.6 2.7 %compare_select_fusion.rows = bf16[288,5625]{1,0:T(8,128)(2,1)S(1)} fusion(bf16[288,5625]{1,0:T(8,128)(2,1)} %param.6, s32[5625]{0:T(1024)S(1)} %dynamic_slice.7, s32[288]{0:T(512)S(1)} %xor.20), kind=kLoop, calls=%fused_computation | loop fusion | flops 3240000 | bytes 6503652 | tf_op jit(solution)/shard_map/jit(_where)/select_n | solution.py:183
  24.3 0.0 collective-permute-done.4.refs_1_
  24.3 0.0 copy-done
  24.4 0.0 copy-done.1
  24.4 2.4 %shard_map.55.refs_3_ = s32[64,2,1280]{2,1,0:T(2,128)S(1)} custom-call(s32[1]{0:T(128)} %bitcast.grp, s32[64]{0:T(128)S(1)} %copy-done.1, bf16[288,5625]{1,0:T(8,128)(2,1)S(1)} %compare_select_fusion.rows, bf16[64,5625]{1,0:T(8,128)(2,1)S(1)} %bitcast.6, bf16[64,5625]{1,0:T(8,128)(2,1)S(1)} %collective-permute-done.4.refs_1_, ...), custom_call_target="tpu_custom_call" | custom-call | flops 2488320000 | bytes 5400000 | tf_op jit(solution)/shard_map/pallas_call | solution.py:129
  26.8 0.0 collective-permute-done.3.refs_0_
  26.8 1.9 %collective-permute-start.5 = (bf16[64,5625]{1,0:T(8,128)(2,1)S(1)}, bf16[64,5625]{1,0:T(8,128)(2,1)S(1)}, u32[]{:S(2)}, u32[]{:S(2)}) collective-permute-start(bf16[64,5625]{1,0:T(8,128)(2,1)S(1)} %collective-permute-done.refs_2_), channel_id=1, source_target_pairs={{0,64},{64,0},{128,192},{192,128},{256,320},{320,256},{384,448},{4... | collective-permute-start | bytes 2160008 | tf_op jit(solution)/shard_map/ppermute | solution.py:52
  28.7 2.4 %collective-permute-start.6 = (bf16[64,5625]{1,0:T(8,128)(2,1)S(1)}, bf16[64,5625]{1,0:T(8,128)(2,1)S(1)}, u32[]{:S(2)}, u32[]{:S(2)}) collective-permute-start(bf16[64,5625]{1,0:T(8,128)(2,1)S(1)} %collective-permute-done.3.refs_0_), channel_id=1, source_target_pairs={{0,64},{64,0},{128,192},{192,128},{256,320},{320,256},{384,448},{4... | collective-permute-start | bytes 2160008 | tf_op jit(solution)/shard_map/ppermute | solution.py:52
  31.1 1.2 %collective-permute-done.1.refs_0_ = bf16[64,5625]{1,0:T(8,128)(2,1)S(1)} collective-permute-done((bf16[64,5625]{1,0:T(8,128)(2,1)S(1)}, bf16[64,5625]{1,0:T(8,128)(2,1)S(1)}, u32[]{:S(2)}, u32[]{:S(2)}) %collective-permute-start.1) | collective-permute-done | bytes 720032 | tf_op jit(solution)/shard_map/ppermute | solution.py:48
  32.3 1.9 %collective-permute-start.2 = (bf16[64,5625]{1,0:T(8,128)(2,1)S(1)}, bf16[64,5625]{1,0:T(8,128)(2,1)S(1)}, u32[]{:S(2)}, u32[]{:S(2)}) collective-permute-start(bf16[64,5625]{1,0:T(8,128)(2,1)S(1)} %collective-permute-done.1.refs_0_), channel_id=1, source_target_pairs={{0,64},{64,0},{128,192},{192,128},{256,320},{320,256},{384,448},{4... | collective-permute-start | bytes 2160008 | tf_op jit(solution)/shard_map/ppermute | solution.py:52
  34.2 0.0 collective-permute-done.5.refs_1_
  34.3 0.0 collective-permute-done.6.refs_2_
  34.3 2.4 %shard_map.56.refs_2_ = s32[64,2,1280]{2,1,0:T(2,128)S(1)} custom-call(s32[1]{0:T(128)} %bitcast.grp, s32[64]{0:T(128)S(1)} %copy-done.1, bf16[288,5625]{1,0:T(8,128)(2,1)S(1)} %compare_select_fusion.rows, bf16[64,5625]{1,0:T(8,128)(2,1)S(1)} %collective-permute-done.3.refs_0_, ...), custom_call_target="tpu_custom_call", output_to_operand_aliasing={{}: (6, {})} | custom-call | flops 2488320000 | bytes 5400000 | tf_op jit(solution)/shard_map/pallas_call | solution.py:129
  36.7 0.0 collective-permute-done.2.refs_1_
  36.7 2.2 %shard_map.57 = s32[64,2,1280]{2,1,0:T(2,128)S(1)} custom-call(s32[1]{0:T(128)} %bitcast.grp, s32[64]{0:T(128)S(1)} %copy-done.1, bf16[288,5625]{1,0:T(8,128)(2,1)S(1)} %compare_select_fusion.rows, bf16[64,5625]{1,0:T(8,128)(2,1)S(1)} %collective-permute-done.1.refs_0_, ...), custom_call_target="tpu_custom_call", output_to_operand_aliasing={{}: (5, {})} | custom-call | flops 1658880000 | bytes 4680000 | tf_op jit(solution)/shard_map/pallas_call | solution.py:129
  38.9 0.2 convert_element_type.6
  39.1 31.2 %all_to_all.5 = s16[64,2,1280]{2,1,0:T(2,128)(2,1)S(1)} all-to-all(s16[64,2,1280]{2,1,0:T(2,128)(2,1)S(1)} %convert_element_type.6), channel_id=1, replica_groups=mesh['grp'=8,'ef'=64] {'ef'}, dimensions={0} | all-to-all | bytes 655360 | tf_op jit(solution)/shard_map/all_to_all | solution.py:191
  70.3 0.3 convert_element_type.7.received
  70.7 1.0 %shard_map.58 = f32[8,288]{1,0:T(8,128)} custom-call(s32[64,2,1280]{2,1,0:T(2,128)S(1)} %convert_element_type.7.received), custom_call_target="tpu_custom_call" | custom-call | tf_op jit(solution)/shard_map/pallas_call | solution.py:161
  (1 shorter events, 0.0 us)
Async XLA Ops:
  0.0 15.2 %collective-permute-start = (bf16[64,5625]{1,0:T(8,128)(2,1)}, bf16[64,5625]{1,0:T(8,128)(2,1)S(1)}, u32[]{:S(2)}, u32[]{:S(2)}) collective-permute-start(bf16[64,5625]{1,0:T(8,128)(2,1)} %bitcast.3), channel_id=1, source_target_pairs={{0,128},{64,448},{128,0},{192,320},{256,384},{320,192},{384,256},{... | collective-permute-start | bytes 2160008 | tf_op jit(solution)/shard_map/ppermute | solution.py:48
  6.3 18.1 %collective-permute-start.4 = (bf16[64,5625]{1,0:T(8,128)(2,1)}, bf16[64,5625]{1,0:T(8,128)(2,1)S(1)}, u32[]{:S(2)}, u32[]{:S(2)}) collective-permute-start(bf16[64,5625]{1,0:T(8,128)(2,1)} %bitcast.4), channel_id=1, source_target_pairs={{0,64},{64,0},{128,192},{192,128},{256,320},{320,256},{384,448},{4... | collective-permute-start | bytes 2160008 | tf_op jit(solution)/shard_map/ppermute | solution.py:52
  8.2 18.6 %collective-permute-start.3 = (bf16[64,5625]{1,0:T(8,128)(2,1)}, bf16[64,5625]{1,0:T(8,128)(2,1)S(1)}, u32[]{:S(2)}, u32[]{:S(2)}) collective-permute-start(bf16[64,5625]{1,0:T(8,128)(2,1)} %bitcast.5), channel_id=1, source_target_pairs={{0,384},{64,192},{128,256},{192,64},{256,128},{320,448},{384,0},{4... | collective-permute-start | bytes 2160008 | tf_op jit(solution)/shard_map/ppermute | solution.py:48
  15.1 9.2 %copy-start = (bf16[5625,64]{0,1:T(8,128)(2,1)S(1)}, bf16[5625,64]{0,1:T(8,128)(2,1)}, u32[]{:S(2)}) copy-start(bf16[5625,64]{0,1:T(8,128)(2,1)} %param.5) | copy-start | bytes 2160004
  15.2 9.2 %copy-start.1 = (s32[64]{0:T(128)S(1)}, s32[64]{0:T(128)}, u32[]{:S(2)}) copy-start(s32[64]{0:T(128)} %slot_pair.5) | copy-start | bytes 772
  15.2 17.1 %collective-permute-start.1 = (bf16[64,5625]{1,0:T(8,128)(2,1)S(1)}, bf16[64,5625]{1,0:T(8,128)(2,1)S(1)}, u32[]{:S(2)}, u32[]{:S(2)}) collective-permute-start(bf16[64,5625]{1,0:T(8,128)(2,1)S(1)} %collective-permute-done.refs_2_), channel_id=1, source_target_pairs={{0,384},{64,192},{128,256},{192,64},{256,128},{320,448},{384,0},{4... | collective-permute-start | bytes 2160008 | tf_op jit(solution)/shard_map/ppermute | solution.py:48
  26.8 7.5 %collective-permute-start.5 = (bf16[64,5625]{1,0:T(8,128)(2,1)S(1)}, bf16[64,5625]{1,0:T(8,128)(2,1)S(1)}, u32[]{:S(2)}, u32[]{:S(2)}) collective-permute-start(bf16[64,5625]{1,0:T(8,128)(2,1)S(1)} %collective-permute-done.refs_2_), channel_id=1, source_target_pairs={{0,64},{64,0},{128,192},{192,128},{256,320},{320,256},{384,448},{4... | collective-permute-start | bytes 2160008 | tf_op jit(solution)/shard_map/ppermute | solution.py:52
  28.7 5.6 %collective-permute-start.6 = (bf16[64,5625]{1,0:T(8,128)(2,1)S(1)}, bf16[64,5625]{1,0:T(8,128)(2,1)S(1)}, u32[]{:S(2)}, u32[]{:S(2)}) collective-permute-start(bf16[64,5625]{1,0:T(8,128)(2,1)S(1)} %collective-permute-done.3.refs_0_), channel_id=1, source_target_pairs={{0,64},{64,0},{128,192},{192,128},{256,320},{320,256},{384,448},{4... | collective-permute-start | bytes 2160008 | tf_op jit(solution)/shard_map/ppermute | solution.py:52
  32.3 4.3 %collective-permute-start.2 = (bf16[64,5625]{1,0:T(8,128)(2,1)S(1)}, bf16[64,5625]{1,0:T(8,128)(2,1)S(1)}, u32[]{:S(2)}, u32[]{:S(2)}) collective-permute-start(bf16[64,5625]{1,0:T(8,128)(2,1)S(1)} %collective-permute-done.1.refs_0_), channel_id=1, source_target_pairs={{0,64},{64,0},{128,192},{192,128},{256,320},{320,256},{384,448},{4... | collective-permute-start | bytes 2160008 | tf_op jit(solution)/shard_map/ppermute | solution.py:52

commit v4 on v3

--- a/solution.py
+++ b/solution.py
@@ -29,6 +29,22 @@
     )
 
 
+def copy_kernel(*refs):
+    for source, out in zip(refs[: len(refs) // 2], refs[len(refs) // 2 :], strict=True):
+        out[...] = source[...]
+
+
+def near_copies(*tables):
+    return pl.pallas_call(
+        copy_kernel,
+        out_shape=[jax.ShapeDtypeStruct(t.shape, t.dtype) for t in tables],
+        in_specs=[VMEM] * len(tables),
+        out_specs=[VMEM] * len(tables),
+        compiler_params=pltpu.CompilerParams(vmem_limit_bytes=VMEM_LIMIT),
+        cost_estimate=pl.CostEstimate(flops=0, bytes_accessed=4096, transcendentals=0),
+    )(*tables)
+
+
 def column_symmetry(orbital_irrep, width):
     offset = lax.axis_index("ef") * width
     count = (V - 1 + width) // V + 1
@@ -59,24 +75,21 @@
         span = slice(low, min(low + CHUNK, width))
         left = jnp.concatenate([c[:, span] for c in columns], axis=0)
         part = lax.dot_general(
-            left, rows[:, span], (((1,), (1,)), ((), ())), preferred_element_type=jnp.float32
+            rows[:, span], left, (((1,), (1,)), ((), ())), preferred_element_type=jnp.float32
         )
         total = part if total is None else total + part
-    return total
+    return total.T
 
 
 def pack(out, pair, block, exponent):
-    for j in range(ROOTS // 2):
-        two = slice(2 * j, 2 * j + 2)
-        out[pair, :, j * LANES : (j + 1) * LANES] = block[two, :LANES]
-        out[pair, :, (4 + j) * LANES : (5 + j) * LANES] = block[two, LANES : 2 * LANES]
     lane = lax.broadcasted_iota(jnp.int32, (2, LANES), 1)
     tail = block[:2, 2 * LANES :]
     for j in range(1, ROOTS // 2):
         piece = pltpu.roll(block[2 * j : 2 * j + 2, 2 * LANES :], j * TAIL, 1)
         tail = jnp.where(lane >= j * TAIL, piece, tail)
-    out[pair, :, 8 * LANES : 9 * LANES] = tail
-    out[pair, :, 9 * LANES :] = exponent
+    pieces = [block[2 * j : 2 * j + 2, :LANES] for j in range(ROOTS // 2)]
+    pieces += [block[2 * j : 2 * j + 2, LANES : 2 * LANES] for j in range(ROOTS // 2)]
+    out[pair] = jnp.concatenate(pieces + [tail, exponent], axis=1).astype(out.dtype)
 
 
 def store_slots(grp, slot_pair, owners, held, steps, exponents, out):
@@ -128,7 +141,7 @@
     before = [] if ordered is None else [ordered]
     return pl.pallas_call(
         functools.partial(product_kernel, part),
-        out_shape=jax.ShapeDtypeStruct((slot_pair.shape[0], 2, 10 * LANES), jnp.int32),
+        out_shape=jax.ShapeDtypeStruct((slot_pair.shape[0], 2, 10 * LANES), jnp.int16),
         in_specs=[SMEM, SMEM, VMEM] + [VMEM] * len(columns) + [VMEM] * len(before),
         out_specs=VMEM,
         scratch_shapes=[
@@ -144,9 +157,9 @@
 
 def total_kernel(received, out):
     width = 9 * LANES
-    unit = jnp.exp2(received[:, :, width:].astype(jnp.float32)) * (1.0 / STEPS)
+    unit = jnp.exp2(received[:, :, width:].astype(jnp.int32).astype(jnp.float32)) * (1.0 / STEPS)
     for j in range(9):
-        steps = received[:, :, j * LANES : (j + 1) * LANES].astype(jnp.float32)
+        steps = received[:, :, j * LANES : (j + 1) * LANES].astype(jnp.int32).astype(jnp.float32)
         total = jnp.sum(steps * unit, axis=0)
         if j < 8:
             row = 2 * (j % 4)
@@ -172,6 +185,7 @@
     own = amplitudes.T
     mine = other_chip(own, 0)
 
+    orbital_irrep, panel_rows = near_copies(orbital_irrep, panel_rows)
     col_sym = column_symmetry(orbital_irrep, ladder.shape[1])
     row_sym = jnp.bitwise_xor(
         lookup(panel_rows // V, orbital_irrep), lookup(panel_rows % V, orbital_irrep)
@@ -188,8 +202,8 @@
     ordered = slot_products("second", grp, slot_pair, masked, near, ordered)
     far_other = other_core(far)
     ordered = slot_products("far", grp, slot_pair, masked, (far, far_other), ordered)
-    received = lax.all_to_all(ordered.astype(jnp.int16), "ef", 0, 0, tiled=True)
-    return add_received(received.astype(jnp.int32), ladder.shape[0]).T
+    received = lax.all_to_all(ordered, "ef", 0, 0, tiled=True)
+    return add_received(received, ladder.shape[0]).T
 
 
 def solution(mesh):

time: 73.1 us -> 70.4 us (0.963)
  other arithmetic: 5.81 us -> 3.2 us
  starting transfers between devices: 24.2 us -> 26.1 us
  blocking collectives: 31.2 us -> 29.8 us
  Pallas kernels: 8 us -> 6.81 us
    ppermute x3, starting transfers between devices: 16.1 us -> 18 us  [other_chip(): return lax.ppermute(value, 'grp', pairs)]
    all_to_all x1, blocking collectives: 31.2 us -> 29.8 us  [on_device(): received = lax.all_to_all(ordered, 'ef', 0, 0, tiled=True)]
    unnamed x4 -> x8, local copies, waits for them, and re-layouts: 0.01 us -> 1.37 us
    pallas_call x3, Pallas kernels: 6.97 us -> 5.68 us  [slot_products(): pl.pallas_call(functools.partial(product_kernel, part), out_shape=jax.Sha...]
  transfers between devices with their start and end apart: 7 -> 7, of which waited for: 1 -> 3; matrix products, arithmetic and copies ran while one was open for 9% -> 5% of each run, Pallas kernels for 7% -> 6%
where the time goes in v4:
time: 70.4 us; the launch traced here: 69.1 us
  blocking collectives  29.8 us (42%)
  starting transfers between devices  26.1 us (37%)
  Pallas kernels  6.81 us (10%)
  other arithmetic  3.2 us (5%)
  local copies, waits for them, and re-layouts  1.62 us (2%)
  waiting for transfers between devices  1.31 us (2%)
    all_to_all x1, blocking collectives, on_device(): received = lax.all_to_all(ordered, 'ef', 0, 0, tiled=True)  29.8 us
    ppermute x3, starting transfers between devices, other_chip(): return lax.ppermute(value, 'grp', pairs)  18 us
    ppermute x4, starting transfers between devices, other_core(): return lax.ppermute(value, 'grp', [(g, g ^ 1) for g in range(2 * N_X)])  8.16 us
    pallas_call x3, Pallas kernels, slot_products(): pl.pallas_call(functools.partial(product_kernel, part), out_shape=jax.Sha...  5.68 us
    select_n x1, other arithmetic, on_device(): jnp.where(row_sym[:, None] == col_sym[None, :], ladder, jnp.zeros((), lad...  2.72 us
  transfers between devices with their start and end apart: 7, of which 3 were waited for; matrix products, arithmetic and copies ran while one was open for 5% of the time, Pallas kernels for 6%

profile of v4, /device:TPU:6, one launch (start us, length us, event | category | flops | bytes accessed | tf_op | source)
XLA Modules:
  0.0 69.1 jit_solution(9135989204615918776)
XLA Ops:
  0.0 2.7 %collective-permute-start = (bf16[64,5625]{1,0:T(8,128)(2,1)}, bf16[64,5625]{1,0:T(8,128)(2,1)S(1)}, u32[]{:S(2)}, u32[]{:S(2)}) collective-permute-start(bf16[64,5625]{1,0:T(8,128)(2,1)} %bitcast.3), channel_id=1, source_target_pairs={{0,128},{64,448},{128,0},{192,320},{256,384},{320,192},{384,256},{... | collective-permute-start | bytes 2160008 | tf_op jit(solution)/shard_map/ppermute | solution.py:64
  2.8 0.0 copy-start
  2.8 0.7 copy-done
  3.5 0.7 copy-done.1
  4.1 0.1 pad_dynamic-slice_fusion
  4.2 0.1 broadcast_xor_fusion
  4.3 0.1 xor.24
  4.4 0.1 dynamic_slice.7
  4.5 0.4 select_reduce_fusion
  4.9 1.9 %collective-permute-start.4 = (bf16[64,5625]{1,0:T(8,128)(2,1)}, bf16[64,5625]{1,0:T(8,128)(2,1)S(1)}, u32[]{:S(2)}, u32[]{:S(2)}) collective-permute-start(bf16[64,5625]{1,0:T(8,128)(2,1)} %bitcast.4), channel_id=1, source_target_pairs={{0,64},{64,0},{128,192},{192,128},{256,320},{320,256},{384,448},{4... | collective-permute-start | bytes 2160008 | tf_op jit(solution)/shard_map/ppermute | solution.py:68
  6.8 6.9 %collective-permute-start.3 = (bf16[64,5625]{1,0:T(8,128)(2,1)}, bf16[64,5625]{1,0:T(8,128)(2,1)S(1)}, u32[]{:S(2)}, u32[]{:S(2)}) collective-permute-start(bf16[64,5625]{1,0:T(8,128)(2,1)} %bitcast.5), channel_id=1, source_target_pairs={{0,384},{64,192},{128,256},{192,64},{256,128},{320,448},{384,0},{4... | collective-permute-start | bytes 2160008 | tf_op jit(solution)/shard_map/ppermute | solution.py:64
  13.8 0.0 copy-start.2
  13.8 0.0 copy-start.3
  13.8 0.9 %collective-permute-done.refs_2_ = bf16[64,5625]{1,0:T(8,128)(2,1)S(1)} collective-permute-done((bf16[64,5625]{1,0:T(8,128)(2,1)}, bf16[64,5625]{1,0:T(8,128)(2,1)S(1)}, u32[]{:S(2)}, u32[]{:S(2)}) %collective-permute-start) | collective-permute-done | bytes 720032 | tf_op jit(solution)/shard_map/ppermute | solution.py:64
  14.7 8.3 %collective-permute-start.1 = (bf16[64,5625]{1,0:T(8,128)(2,1)S(1)}, bf16[64,5625]{1,0:T(8,128)(2,1)S(1)}, u32[]{:S(2)}, u32[]{:S(2)}) collective-permute-start(bf16[64,5625]{1,0:T(8,128)(2,1)S(1)} %collective-permute-done.refs_2_), channel_id=1, source_target_pairs={{0,384},{64,192},{128,256},{192,64},{256,128},{320,448},{384,0},{4... | collective-permute-start | bytes 2160008 | tf_op jit(solution)/shard_map/ppermute | solution.py:64
  23.0 2.7 %compare_select_fusion.rows = bf16[288,5625]{1,0:T(8,128)(2,1)S(1)} fusion(bf16[288,5625]{1,0:T(8,128)(2,1)} %param.6, s32[5625]{0:T(1024)S(1)} %dynamic_slice.7, s32[288]{0:T(512)S(1)} %xor.20), kind=kLoop, calls=%fused_computation | loop fusion | flops 3240000 | bytes 6503652 | tf_op jit(solution)/shard_map/jit(_where)/select_n | solution.py:197
  25.7 0.0 collective-permute-done.4.refs_1_
  25.7 0.0 copy-done.2
  25.7 0.0 copy-done.3
  25.7 1.9 %shard_map.56.refs_3_ = s16[64,2,1280]{2,1,0:T(2,128)(2,1)S(1)} custom-call(s32[1]{0:T(128)} %bitcast.grp, s32[64]{0:T(128)S(1)} %copy-done.3, bf16[288,5625]{1,0:T(8,128)(2,1)S(1)} %compare_select_fusion.rows, bf16[64,5625]{1,0:T(8,128)(2,1)S(1)} %bitcast.6, bf16[64,5625]{1,0:T(8,128)(2,1)S(1)} %collective-permute-done.4.refs_1_, ...), custom_call_target="tpu_custom_call" | custom-call | flops 2488320000 | bytes 5400000 | tf_op jit(solution)/shard_map/pallas_call | solution.py:142
  27.6 0.0 collective-permute-done.3.refs_0_
  27.7 1.9 %collective-permute-start.5 = (bf16[64,5625]{1,0:T(8,128)(2,1)S(1)}, bf16[64,5625]{1,0:T(8,128)(2,1)S(1)}, u32[]{:S(2)}, u32[]{:S(2)}) collective-permute-start(bf16[64,5625]{1,0:T(8,128)(2,1)S(1)} %collective-permute-done.refs_2_), channel_id=1, source_target_pairs={{0,64},{64,0},{128,192},{192,128},{256,320},{320,256},{384,448},{4... | collective-permute-start | bytes 2160008 | tf_op jit(solution)/shard_map/ppermute | solution.py:68
  29.6 2.4 %collective-permute-start.6 = (bf16[64,5625]{1,0:T(8,128)(2,1)S(1)}, bf16[64,5625]{1,0:T(8,128)(2,1)S(1)}, u32[]{:S(2)}, u32[]{:S(2)}) collective-permute-start(bf16[64,5625]{1,0:T(8,128)(2,1)S(1)} %collective-permute-done.3.refs_0_), channel_id=1, source_target_pairs={{0,64},{64,0},{128,192},{192,128},{256,320},{320,256},{384,448},{4... | collective-permute-start | bytes 2160008 | tf_op jit(solution)/shard_map/ppermute | solution.py:68
  32.0 0.2 collective-permute-done.1.refs_0_
  32.2 1.9 %collective-permute-start.2 = (bf16[64,5625]{1,0:T(8,128)(2,1)S(1)}, bf16[64,5625]{1,0:T(8,128)(2,1)S(1)}, u32[]{:S(2)}, u32[]{:S(2)}) collective-permute-start(bf16[64,5625]{1,0:T(8,128)(2,1)S(1)} %collective-permute-done.1.refs_0_), channel_id=1, source_target_pairs={{0,64},{64,0},{128,192},{192,128},{256,320},{320,256},{384,448},{4... | collective-permute-start | bytes 2160008 | tf_op jit(solution)/shard_map/ppermute | solution.py:68
  34.1 0.0 collective-permute-done.5.refs_1_
  34.1 0.0 collective-permute-done.6.refs_2_
  34.2 1.9 %shard_map.57.refs_2_ = s16[64,2,1280]{2,1,0:T(2,128)(2,1)S(1)} custom-call(s32[1]{0:T(128)} %bitcast.grp, s32[64]{0:T(128)S(1)} %copy-done.3, bf16[288,5625]{1,0:T(8,128)(2,1)S(1)} %compare_select_fusion.rows, bf16[64,5625]{1,0:T(8,128)(2,1)S(1)} %collective-permute-done.3.refs_0_, ...), custom_call_target="tpu_custom_call", output_to_operand_aliasing={{}: (6, {})} | custom-call | flops 2488320000 | bytes 5400000 | tf_op jit(solution)/shard_map/pallas_call | solution.py:142
  36.1 0.2 collective-permute-done.2.refs_1_
  36.3 1.8 %shard_map.58 = s16[64,2,1280]{2,1,0:T(2,128)(2,1)S(1)} custom-call(s32[1]{0:T(128)} %bitcast.grp, s32[64]{0:T(128)S(1)} %copy-done.3, bf16[288,5625]{1,0:T(8,128)(2,1)S(1)} %compare_select_fusion.rows, bf16[64,5625]{1,0:T(8,128)(2,1)S(1)} %collective-permute-done.1.refs_0_, ...), custom_call_target="tpu_custom_call", output_to_operand_aliasing={{}: (5, {})} | custom-call | flops 1658880000 | bytes 4680000 | tf_op jit(solution)/shard_map/pallas_call | solution.py:142
  38.1 29.8 %all_to_all.5.received = s16[64,2,1280]{2,1,0:T(2,128)(2,1)S(1)} all-to-all(s16[64,2,1280]{2,1,0:T(2,128)(2,1)S(1)} %shard_map.58), channel_id=1, replica_groups=mesh['grp'=8,'ef'=64] {'ef'}, dimensions={0} | all-to-all | bytes 655360 | tf_op jit(solution)/shard_map/all_to_all | solution.py:205
  67.9 1.1 %shard_map.59 = f32[8,288]{1,0:T(8,128)} custom-call(s16[64,2,1280]{2,1,0:T(2,128)(2,1)S(1)} %all_to_all.5.received), custom_call_target="tpu_custom_call" | custom-call | tf_op jit(solution)/shard_map/pallas_call | solution.py:174
  (4 shorter events, 0.0 us)
Async XLA Ops:
  0.0 14.7 %collective-permute-start = (bf16[64,5625]{1,0:T(8,128)(2,1)}, bf16[64,5625]{1,0:T(8,128)(2,1)S(1)}, u32[]{:S(2)}, u32[]{:S(2)}) collective-permute-start(bf16[64,5625]{1,0:T(8,128)(2,1)} %bitcast.3), channel_id=1, source_target_pairs={{0,128},{64,448},{128,0},{192,320},{256,384},{320,192},{384,256},{... | collective-permute-start | bytes 2160008 | tf_op jit(solution)/shard_map/ppermute | solution.py:64
  2.8 0.7 copy-start
  3.5 0.7 copy-start.1
  4.9 20.8 %collective-permute-start.4 = (bf16[64,5625]{1,0:T(8,128)(2,1)}, bf16[64,5625]{1,0:T(8,128)(2,1)S(1)}, u32[]{:S(2)}, u32[]{:S(2)}) collective-permute-start(bf16[64,5625]{1,0:T(8,128)(2,1)} %bitcast.4), channel_id=1, source_target_pairs={{0,64},{64,0},{128,192},{192,128},{256,320},{320,256},{384,448},{4... | collective-permute-start | bytes 2160008 | tf_op jit(solution)/shard_map/ppermute | solution.py:68
  6.8 20.8 %collective-permute-start.3 = (bf16[64,5625]{1,0:T(8,128)(2,1)}, bf16[64,5625]{1,0:T(8,128)(2,1)S(1)}, u32[]{:S(2)}, u32[]{:S(2)}) collective-permute-start(bf16[64,5625]{1,0:T(8,128)(2,1)} %bitcast.5), channel_id=1, source_target_pairs={{0,384},{64,192},{128,256},{192,64},{256,128},{320,448},{384,0},{4... | collective-permute-start | bytes 2160008 | tf_op jit(solution)/shard_map/ppermute | solution.py:64
  13.8 11.9 %copy-start.2 = (bf16[5625,64]{0,1:T(8,128)(2,1)S(1)}, bf16[5625,64]{0,1:T(8,128)(2,1)}, u32[]{:S(2)}) copy-start(bf16[5625,64]{0,1:T(8,128)(2,1)} %param.5) | copy-start | bytes 2160004
  13.8 11.9 %copy-start.3 = (s32[64]{0:T(128)S(1)}, s32[64]{0:T(128)}, u32[]{:S(2)}) copy-start(s32[64]{0:T(128)} %slot_pair.5) | copy-start | bytes 772
  14.7 17.5 %collective-permute-start.1 = (bf16[64,5625]{1,0:T(8,128)(2,1)S(1)}, bf16[64,5625]{1,0:T(8,128)(2,1)S(1)}, u32[]{:S(2)}, u32[]{:S(2)}) collective-permute-start(bf16[64,5625]{1,0:T(8,128)(2,1)S(1)} %collective-permute-done.refs_2_), channel_id=1, source_target_pairs={{0,384},{64,192},{128,256},{192,64},{256,128},{320,448},{384,0},{4... | collective-permute-start | bytes 2160008 | tf_op jit(solution)/shard_map/ppermute | solution.py:64
  27.7 6.5 %collective-permute-start.5 = (bf16[64,5625]{1,0:T(8,128)(2,1)S(1)}, bf16[64,5625]{1,0:T(8,128)(2,1)S(1)}, u32[]{:S(2)}, u32[]{:S(2)}) collective-permute-start(bf16[64,5625]{1,0:T(8,128)(2,1)S(1)} %collective-permute-done.refs_2_), channel_id=1, source_target_pairs={{0,64},{64,0},{128,192},{192,128},{256,320},{320,256},{384,448},{4... | collective-permute-start | bytes 2160008 | tf_op jit(solution)/shard_map/ppermute | solution.py:68
  29.6 4.6 %collective-permute-start.6 = (bf16[64,5625]{1,0:T(8,128)(2,1)S(1)}, bf16[64,5625]{1,0:T(8,128)(2,1)S(1)}, u32[]{:S(2)}, u32[]{:S(2)}) collective-permute-start(bf16[64,5625]{1,0:T(8,128)(2,1)S(1)} %collective-permute-done.3.refs_0_), channel_id=1, source_target_pairs={{0,64},{64,0},{128,192},{192,128},{256,320},{320,256},{384,448},{4... | collective-permute-start | bytes 2160008 | tf_op jit(solution)/shard_map/ppermute | solution.py:68
  32.2 4.1 %collective-permute-start.2 = (bf16[64,5625]{1,0:T(8,128)(2,1)S(1)}, bf16[64,5625]{1,0:T(8,128)(2,1)S(1)}, u32[]{:S(2)}, u32[]{:S(2)}) collective-permute-start(bf16[64,5625]{1,0:T(8,128)(2,1)S(1)} %collective-permute-done.1.refs_0_), channel_id=1, source_target_pairs={{0,64},{64,0},{128,192},{192,128},{256,320},{320,256},{384,448},{4... | collective-permute-start | bytes 2160008 | tf_op jit(solution)/shard_map/ppermute | solution.py:68

commit v5 on v4

--- a/solution.py
+++ b/solution.py
@@ -157,17 +157,19 @@
 
 def total_kernel(received, out):
     width = 9 * LANES
-    unit = jnp.exp2(received[:, :, width:].astype(jnp.int32).astype(jnp.float32)) * (1.0 / STEPS)
-    for j in range(9):
-        steps = received[:, :, j * LANES : (j + 1) * LANES].astype(jnp.int32).astype(jnp.float32)
-        total = jnp.sum(steps * unit, axis=0)
-        if j < 8:
-            row = 2 * (j % 4)
-            out[row : row + 2, j // 4 * LANES : (j // 4 + 1) * LANES] = total
-        else:
-            for i in range(ROOTS // 2):
-                tail = total if i == 0 else pltpu.roll(total, LANES - i * TAIL, 1)
-                out[2 * i : 2 * i + 2, 2 * LANES :] = tail[:, :TAIL]
+    total = jnp.zeros((2, width), jnp.float32)
+    for sender in range(received.shape[0]):
+        exponent = received[sender, :, width:].astype(jnp.int32).astype(jnp.float32)
+        unit = jnp.concatenate([jnp.exp2(exponent) * (1.0 / STEPS)] * 9, axis=1)
+        steps = received[sender, :, :width].astype(jnp.int32).astype(jnp.float32)
+        total = total + steps * unit
+    for j in range(ROOTS // 2):
+        two = slice(2 * j, 2 * j + 2)
+        out[two, :LANES] = total[:, j * LANES : (j + 1) * LANES]
+        out[two, LANES : 2 * LANES] = total[:, (4 + j) * LANES : (5 + j) * LANES]
+        tail = total[:, 8 * LANES :]
+        tail = tail if j == 0 else pltpu.roll(tail, LANES - j * TAIL, 1)
+        out[two, 2 * LANES :] = tail[:, :TAIL]
 
 
 def add_received(received, rows):

time: 70.4 us -> 70.1 us (level)
  no operation moved by 1% of the time
where the time goes in v5:
time: 70.1 us; the launch traced here: 68.7 us
  blocking collectives  29.8 us (43%)
  starting transfers between devices  26.1 us (37%)
  Pallas kernels  6.46 us (9%)
  other arithmetic  3.2 us (5%)
  local copies, waits for them, and re-layouts  1.62 us (2%)
  waiting for transfers between devices  1.31 us (2%)
    all_to_all x1, blocking collectives, on_device(): received = lax.all_to_all(ordered, 'ef', 0, 0, tiled=True)  29.8 us
    ppermute x3, starting transfers between devices, other_chip(): return lax.ppermute(value, 'grp', pairs)  18 us
    ppermute x4, starting transfers between devices, other_core(): return lax.ppermute(value, 'grp', [(g, g ^ 1) for g in range(2 * N_X)])  8.16 us
    pallas_call x3, Pallas kernels, slot_products(): pl.pallas_call(functools.partial(product_kernel, part), out_shape=jax.Sha...  5.68 us
    select_n x1, other arithmetic, on_device(): jnp.where(row_sym[:, None] == col_sym[None, :], ladder, jnp.zeros((), lad...  2.72 us
  transfers between devices with their start and end apart: 7, of which 3 were waited for; matrix products, arithmetic and copies ran while one was open for 5% of the time, Pallas kernels for 6%

profile of v5, /device:TPU:6, one launch (start us, length us, event | category | flops | bytes accessed | tf_op | source)
XLA Modules:
  0.0 68.7 jit_solution(14333851099508217329)
XLA Ops:
  0.0 2.7 %collective-permute-start = (bf16[64,5625]{1,0:T(8,128)(2,1)}, bf16[64,5625]{1,0:T(8,128)(2,1)S(1)}, u32[]{:S(2)}, u32[]{:S(2)}) collective-permute-start(bf16[64,5625]{1,0:T(8,128)(2,1)} %bitcast.3), channel_id=1, source_target_pairs={{0,128},{64,448},{128,0},{192,320},{256,384},{320,192},{384,256},{... | collective-permute-start | bytes 2160008 | tf_op jit(solution)/shard_map/ppermute | solution.py:64
  2.8 0.0 copy-start
  2.8 0.7 copy-done
  3.5 0.7 copy-done.1
  4.1 0.1 pad_dynamic-slice_fusion
  4.2 0.1 broadcast_xor_fusion
  4.3 0.1 xor.24
  4.4 0.1 dynamic_slice.7
  4.5 0.4 select_reduce_fusion
  4.9 1.9 %collective-permute-start.4 = (bf16[64,5625]{1,0:T(8,128)(2,1)}, bf16[64,5625]{1,0:T(8,128)(2,1)S(1)}, u32[]{:S(2)}, u32[]{:S(2)}) collective-permute-start(bf16[64,5625]{1,0:T(8,128)(2,1)} %bitcast.4), channel_id=1, source_target_pairs={{0,64},{64,0},{128,192},{192,128},{256,320},{320,256},{384,448},{4... | collective-permute-start | bytes 2160008 | tf_op jit(solution)/shard_map/ppermute | solution.py:68
  6.8 6.9 %collective-permute-start.3 = (bf16[64,5625]{1,0:T(8,128)(2,1)}, bf16[64,5625]{1,0:T(8,128)(2,1)S(1)}, u32[]{:S(2)}, u32[]{:S(2)}) collective-permute-start(bf16[64,5625]{1,0:T(8,128)(2,1)} %bitcast.5), channel_id=1, source_target_pairs={{0,384},{64,192},{128,256},{192,64},{256,128},{320,448},{384,0},{4... | collective-permute-start | bytes 2160008 | tf_op jit(solution)/shard_map/ppermute | solution.py:64
  13.8 0.0 copy-start.2
  13.8 0.0 copy-start.3
  13.8 0.9 %collective-permute-done.refs_2_ = bf16[64,5625]{1,0:T(8,128)(2,1)S(1)} collective-permute-done((bf16[64,5625]{1,0:T(8,128)(2,1)}, bf16[64,5625]{1,0:T(8,128)(2,1)S(1)}, u32[]{:S(2)}, u32[]{:S(2)}) %collective-permute-start) | collective-permute-done | bytes 720032 | tf_op jit(solution)/shard_map/ppermute | solution.py:64
  14.7 8.3 %collective-permute-start.1 = (bf16[64,5625]{1,0:T(8,128)(2,1)S(1)}, bf16[64,5625]{1,0:T(8,128)(2,1)S(1)}, u32[]{:S(2)}, u32[]{:S(2)}) collective-permute-start(bf16[64,5625]{1,0:T(8,128)(2,1)S(1)} %collective-permute-done.refs_2_), channel_id=1, source_target_pairs={{0,384},{64,192},{128,256},{192,64},{256,128},{320,448},{384,0},{4... | collective-permute-start | bytes 2160008 | tf_op jit(solution)/shard_map/ppermute | solution.py:64
  23.0 2.7 %compare_select_fusion.rows = bf16[288,5625]{1,0:T(8,128)(2,1)S(1)} fusion(bf16[288,5625]{1,0:T(8,128)(2,1)} %param.6, s32[5625]{0:T(1024)S(1)} %dynamic_slice.7, s32[288]{0:T(512)S(1)} %xor.20), kind=kLoop, calls=%fused_computation | loop fusion | flops 3240000 | bytes 6503652 | tf_op jit(solution)/shard_map/jit(_where)/select_n | solution.py:199
  25.7 0.0 collective-permute-done.4.refs_1_
  25.7 0.0 copy-done.2
  25.7 0.0 copy-done.3
  25.7 1.9 %shard_map.56.refs_3_ = s16[64,2,1280]{2,1,0:T(2,128)(2,1)S(1)} custom-call(s32[1]{0:T(128)} %bitcast.grp, s32[64]{0:T(128)S(1)} %copy-done.3, bf16[288,5625]{1,0:T(8,128)(2,1)S(1)} %compare_select_fusion.rows, bf16[64,5625]{1,0:T(8,128)(2,1)S(1)} %bitcast.6, bf16[64,5625]{1,0:T(8,128)(2,1)S(1)} %collective-permute-done.4.refs_1_, ...), custom_call_target="tpu_custom_call" | custom-call | flops 2488320000 | bytes 5400000 | tf_op jit(solution)/shard_map/pallas_call | solution.py:142
  27.6 0.0 collective-permute-done.3.refs_0_
  27.7 1.9 %collective-permute-start.5 = (bf16[64,5625]{1,0:T(8,128)(2,1)S(1)}, bf16[64,5625]{1,0:T(8,128)(2,1)S(1)}, u32[]{:S(2)}, u32[]{:S(2)}) collective-permute-start(bf16[64,5625]{1,0:T(8,128)(2,1)S(1)} %collective-permute-done.refs_2_), channel_id=1, source_target_pairs={{0,64},{64,0},{128,192},{192,128},{256,320},{320,256},{384,448},{4... | collective-permute-start | bytes 2160008 | tf_op jit(solution)/shard_map/ppermute | solution.py:68
  29.6 2.4 %collective-permute-start.6 = (bf16[64,5625]{1,0:T(8,128)(2,1)S(1)}, bf16[64,5625]{1,0:T(8,128)(2,1)S(1)}, u32[]{:S(2)}, u32[]{:S(2)}) collective-permute-start(bf16[64,5625]{1,0:T(8,128)(2,1)S(1)} %collective-permute-done.3.refs_0_), channel_id=1, source_target_pairs={{0,64},{64,0},{128,192},{192,128},{256,320},{320,256},{384,448},{4... | collective-permute-start | bytes 2160008 | tf_op jit(solution)/shard_map/ppermute | solution.py:68
  32.0 0.2 collective-permute-done.1.refs_0_
  32.2 1.9 %collective-permute-start.2 = (bf16[64,5625]{1,0:T(8,128)(2,1)S(1)}, bf16[64,5625]{1,0:T(8,128)(2,1)S(1)}, u32[]{:S(2)}, u32[]{:S(2)}) collective-permute-start(bf16[64,5625]{1,0:T(8,128)(2,1)S(1)} %collective-permute-done.1.refs_0_), channel_id=1, source_target_pairs={{0,64},{64,0},{128,192},{192,128},{256,320},{320,256},{384,448},{4... | collective-permute-start | bytes 2160008 | tf_op jit(solution)/shard_map/ppermute | solution.py:68
  34.1 0.0 collective-permute-done.5.refs_1_
  34.1 0.0 collective-permute-done.6.refs_2_
  34.2 1.9 %shard_map.57.refs_2_ = s16[64,2,1280]{2,1,0:T(2,128)(2,1)S(1)} custom-call(s32[1]{0:T(128)} %bitcast.grp, s32[64]{0:T(128)S(1)} %copy-done.3, bf16[288,5625]{1,0:T(8,128)(2,1)S(1)} %compare_select_fusion.rows, bf16[64,5625]{1,0:T(8,128)(2,1)S(1)} %collective-permute-done.3.refs_0_, ...), custom_call_target="tpu_custom_call", output_to_operand_aliasing={{}: (6, {})} | custom-call | flops 2488320000 | bytes 5400000 | tf_op jit(solution)/shard_map/pallas_call | solution.py:142
  36.1 0.2 collective-permute-done.2.refs_1_
  36.3 1.8 %shard_map.58 = s16[64,2,1280]{2,1,0:T(2,128)(2,1)S(1)} custom-call(s32[1]{0:T(128)} %bitcast.grp, s32[64]{0:T(128)S(1)} %copy-done.3, bf16[288,5625]{1,0:T(8,128)(2,1)S(1)} %compare_select_fusion.rows, bf16[64,5625]{1,0:T(8,128)(2,1)S(1)} %collective-permute-done.1.refs_0_, ...), custom_call_target="tpu_custom_call", output_to_operand_aliasing={{}: (5, {})} | custom-call | flops 1658880000 | bytes 4680000 | tf_op jit(solution)/shard_map/pallas_call | solution.py:142
  38.1 29.8 %all_to_all.5.received = s16[64,2,1280]{2,1,0:T(2,128)(2,1)S(1)} all-to-all(s16[64,2,1280]{2,1,0:T(2,128)(2,1)S(1)} %shard_map.58), channel_id=1, replica_groups=mesh['grp'=8,'ef'=64] {'ef'}, dimensions={0} | all-to-all | bytes 655360 | tf_op jit(solution)/shard_map/all_to_all | solution.py:207
  67.9 0.8 %shard_map.59 = f32[8,288]{1,0:T(8,128)} custom-call(s16[64,2,1280]{2,1,0:T(2,128)(2,1)S(1)} %all_to_all.5.received), custom_call_target="tpu_custom_call" | custom-call | tf_op jit(solution)/shard_map/pallas_call | solution.py:176
  (4 shorter events, 0.0 us)
Async XLA Ops:
  0.0 14.7 %collective-permute-start = (bf16[64,5625]{1,0:T(8,128)(2,1)}, bf16[64,5625]{1,0:T(8,128)(2,1)S(1)}, u32[]{:S(2)}, u32[]{:S(2)}) collective-permute-start(bf16[64,5625]{1,0:T(8,128)(2,1)} %bitcast.3), channel_id=1, source_target_pairs={{0,128},{64,448},{128,0},{192,320},{256,384},{320,192},{384,256},{... | collective-permute-start | bytes 2160008 | tf_op jit(solution)/shard_map/ppermute | solution.py:64
  2.8 0.7 %copy-start = (s32[600]{0:T(1024)S(1)}, s32[600]{0:T(1024)}, u32[]{:S(2)}) copy-start(s32[600]{0:T(1024)} %refs_0_.1) | copy-start | bytes 7204
  3.5 0.7 copy-start.1
  4.9 20.8 %collective-permute-start.4 = (bf16[64,5625]{1,0:T(8,128)(2,1)}, bf16[64,5625]{1,0:T(8,128)(2,1)S(1)}, u32[]{:S(2)}, u32[]{:S(2)}) collective-permute-start(bf16[64,5625]{1,0:T(8,128)(2,1)} %bitcast.4), channel_id=1, source_target_pairs={{0,64},{64,0},{128,192},{192,128},{256,320},{320,256},{384,448},{4... | collective-permute-start | bytes 2160008 | tf_op jit(solution)/shard_map/ppermute | solution.py:68
  6.8 20.8 %collective-permute-start.3 = (bf16[64,5625]{1,0:T(8,128)(2,1)}, bf16[64,5625]{1,0:T(8,128)(2,1)S(1)}, u32[]{:S(2)}, u32[]{:S(2)}) collective-permute-start(bf16[64,5625]{1,0:T(8,128)(2,1)} %bitcast.5), channel_id=1, source_target_pairs={{0,384},{64,192},{128,256},{192,64},{256,128},{320,448},{384,0},{4... | collective-permute-start | bytes 2160008 | tf_op jit(solution)/shard_map/ppermute | solution.py:64
  13.8 11.9 %copy-start.2 = (bf16[5625,64]{0,1:T(8,128)(2,1)S(1)}, bf16[5625,64]{0,1:T(8,128)(2,1)}, u32[]{:S(2)}) copy-start(bf16[5625,64]{0,1:T(8,128)(2,1)} %param.5) | copy-start | bytes 2160004
  13.8 11.9 %copy-start.3 = (s32[64]{0:T(128)S(1)}, s32[64]{0:T(128)}, u32[]{:S(2)}) copy-start(s32[64]{0:T(128)} %slot_pair.5) | copy-start | bytes 772
  14.7 17.5 %collective-permute-start.1 = (bf16[64,5625]{1,0:T(8,128)(2,1)S(1)}, bf16[64,5625]{1,0:T(8,128)(2,1)S(1)}, u32[]{:S(2)}, u32[]{:S(2)}) collective-permute-start(bf16[64,5625]{1,0:T(8,128)(2,1)S(1)} %collective-permute-done.refs_2_), channel_id=1, source_target_pairs={{0,384},{64,192},{128,256},{192,64},{256,128},{320,448},{384,0},{4... | collective-permute-start | bytes 2160008 | tf_op jit(solution)/shard_map/ppermute | solution.py:64
  27.7 6.5 %collective-permute-start.5 = (bf16[64,5625]{1,0:T(8,128)(2,1)S(1)}, bf16[64,5625]{1,0:T(8,128)(2,1)S(1)}, u32[]{:S(2)}, u32[]{:S(2)}) collective-permute-start(bf16[64,5625]{1,0:T(8,128)(2,1)S(1)} %collective-permute-done.refs_2_), channel_id=1, source_target_pairs={{0,64},{64,0},{128,192},{192,128},{256,320},{320,256},{384,448},{4... | collective-permute-start | bytes 2160008 | tf_op jit(solution)/shard_map/ppermute | solution.py:68
  29.6 4.6 %collective-permute-start.6 = (bf16[64,5625]{1,0:T(8,128)(2,1)S(1)}, bf16[64,5625]{1,0:T(8,128)(2,1)S(1)}, u32[]{:S(2)}, u32[]{:S(2)}) collective-permute-start(bf16[64,5625]{1,0:T(8,128)(2,1)S(1)} %collective-permute-done.3.refs_0_), channel_id=1, source_target_pairs={{0,64},{64,0},{128,192},{192,128},{256,320},{320,256},{384,448},{4... | collective-permute-start | bytes 2160008 | tf_op jit(solution)/shard_map/ppermute | solution.py:68
  32.2 4.1 %collective-permute-start.2 = (bf16[64,5625]{1,0:T(8,128)(2,1)S(1)}, bf16[64,5625]{1,0:T(8,128)(2,1)S(1)}, u32[]{:S(2)}, u32[]{:S(2)}) collective-permute-start(bf16[64,5625]{1,0:T(8,128)(2,1)S(1)} %collective-permute-done.1.refs_0_), channel_id=1, source_target_pairs={{0,64},{64,0},{128,192},{192,128},{256,320},{320,256},{384,448},{4... | collective-permute-start | bytes 2160008 | tf_op jit(solution)/shard_map/ppermute | solution.py:68

commit v6 on v5

--- a/solution.py
+++ b/solution.py
@@ -15,6 +15,9 @@
 LANES = 128
 TAIL = 32
 STEPS = 32000.0
+PAIRS = 64
+STRIDE = 25
+PLACE = pow(STRIDE, -1, PAIRS)
 SMALLEST = 1e-30
 VMEM_LIMIT = 10 << 20
 
@@ -103,7 +106,7 @@
     for block, (chip, core) in enumerate(owners):
         group = lax.rem(chip, N_X) * 2 + core
         for slot in range(GROUP_SLOTS):
-            pair = slot_pair[group * GROUP_SLOTS + slot]
+            pair = lax.rem(slot_pair[group * GROUP_SLOTS + slot] * PLACE, PAIRS)
             index = block * GROUP_SLOTS + slot
             pack(out, pair, steps[index], exponents[index])
 
@@ -204,7 +207,8 @@
     ordered = slot_products("second", grp, slot_pair, masked, near, ordered)
     far_other = other_core(far)
     ordered = slot_products("far", grp, slot_pair, masked, (far, far_other), ordered)
-    received = lax.all_to_all(ordered, "ef", 0, 0, tiled=True)
+    members = [[i * STRIDE % PAIRS for i in range(PAIRS)]]
+    received = lax.all_to_all(ordered, "ef", 0, 0, tiled=True, axis_index_groups=members)
     return add_received(received, ladder.shape[0]).T
 
 

time: 70.1 us -> 69.2 us (0.987)
  no operation moved by 1% of the time
where the time goes in v6:
time: 69.2 us; the launch traced here: 68 us
  blocking collectives  29.1 us (42%)
  starting transfers between devices  26.1 us (38%)
  Pallas kernels  6.47 us (9%)
  other arithmetic  3.2 us (5%)
  local copies, waits for them, and re-layouts  1.62 us (2%)
  waiting for transfers between devices  1.3 us (2%)
    all_to_all x1, blocking collectives, on_device(): lax.all_to_all(ordered, 'ef', 0, 0, tiled=True, axis_index_groups=members)  29.1 us
    ppermute x3, starting transfers between devices, other_chip(): return lax.ppermute(value, 'grp', pairs)  18 us
    ppermute x4, starting transfers between devices, other_core(): return lax.ppermute(value, 'grp', [(g, g ^ 1) for g in range(2 * N_X)])  8.16 us
    pallas_call x3, Pallas kernels, slot_products(): pl.pallas_call(functools.partial(product_kernel, part), out_shape=jax.Sha...  5.68 us
    select_n x1, other arithmetic, on_device(): jnp.where(row_sym[:, None] == col_sym[None, :], ladder, jnp.zeros((), lad...  2.72 us
  transfers between devices with their start and end apart: 7, of which 3 were waited for; matrix products, arithmetic and copies ran while one was open for 5% of the time, Pallas kernels for 6%

profile of v6, /device:TPU:6, one launch (start us, length us, event | category | flops | bytes accessed | tf_op | source)
XLA Modules:
  0.0 68.0 jit_solution(16233137335967367914)
XLA Ops:
  0.0 2.7 %collective-permute-start = (bf16[64,5625]{1,0:T(8,128)(2,1)}, bf16[64,5625]{1,0:T(8,128)(2,1)S(1)}, u32[]{:S(2)}, u32[]{:S(2)}) collective-permute-start(bf16[64,5625]{1,0:T(8,128)(2,1)} %bitcast.3), channel_id=1, source_target_pairs={{0,128},{64,448},{128,0},{192,320},{256,384},{320,192},{384,256},{... | collective-permute-start | bytes 2160008 | tf_op jit(solution)/shard_map/ppermute | solution.py:67
  2.8 0.0 copy-start
  2.8 0.7 copy-done
  3.5 0.7 copy-done.1
  4.1 0.1 pad_dynamic-slice_fusion
  4.2 0.1 broadcast_xor_fusion
  4.3 0.1 xor.24
  4.4 0.1 dynamic_slice.7
  4.5 0.4 select_reduce_fusion
  4.9 1.9 %collective-permute-start.4 = (bf16[64,5625]{1,0:T(8,128)(2,1)}, bf16[64,5625]{1,0:T(8,128)(2,1)S(1)}, u32[]{:S(2)}, u32[]{:S(2)}) collective-permute-start(bf16[64,5625]{1,0:T(8,128)(2,1)} %bitcast.4), channel_id=1, source_target_pairs={{0,64},{64,0},{128,192},{192,128},{256,320},{320,256},{384,448},{4... | collective-permute-start | bytes 2160008 | tf_op jit(solution)/shard_map/ppermute | solution.py:71
  6.8 6.9 %collective-permute-start.3 = (bf16[64,5625]{1,0:T(8,128)(2,1)}, bf16[64,5625]{1,0:T(8,128)(2,1)S(1)}, u32[]{:S(2)}, u32[]{:S(2)}) collective-permute-start(bf16[64,5625]{1,0:T(8,128)(2,1)} %bitcast.5), channel_id=1, source_target_pairs={{0,384},{64,192},{128,256},{192,64},{256,128},{320,448},{384,0},{4... | collective-permute-start | bytes 2160008 | tf_op jit(solution)/shard_map/ppermute | solution.py:67
  13.8 0.0 copy-start.2
  13.8 0.0 copy-start.3
  13.8 0.9 %collective-permute-done.refs_2_ = bf16[64,5625]{1,0:T(8,128)(2,1)S(1)} collective-permute-done((bf16[64,5625]{1,0:T(8,128)(2,1)}, bf16[64,5625]{1,0:T(8,128)(2,1)S(1)}, u32[]{:S(2)}, u32[]{:S(2)}) %collective-permute-start) | collective-permute-done | bytes 720032 | tf_op jit(solution)/shard_map/ppermute | solution.py:67
  14.7 8.3 %collective-permute-start.1 = (bf16[64,5625]{1,0:T(8,128)(2,1)S(1)}, bf16[64,5625]{1,0:T(8,128)(2,1)S(1)}, u32[]{:S(2)}, u32[]{:S(2)}) collective-permute-start(bf16[64,5625]{1,0:T(8,128)(2,1)S(1)} %collective-permute-done.refs_2_), channel_id=1, source_target_pairs={{0,384},{64,192},{128,256},{192,64},{256,128},{320,448},{384,0},{4... | collective-permute-start | bytes 2160008 | tf_op jit(solution)/shard_map/ppermute | solution.py:67
  23.0 2.7 %compare_select_fusion.rows = bf16[288,5625]{1,0:T(8,128)(2,1)S(1)} fusion(bf16[288,5625]{1,0:T(8,128)(2,1)} %param.6, s32[5625]{0:T(1024)S(1)} %dynamic_slice.7, s32[288]{0:T(512)S(1)} %xor.20), kind=kLoop, calls=%fused_computation | loop fusion | flops 3240000 | bytes 6503652 | tf_op jit(solution)/shard_map/jit(_where)/select_n | solution.py:202
  25.7 0.0 collective-permute-done.4.refs_1_
  25.7 0.0 copy-done.2
  25.7 0.0 copy-done.3
  25.7 1.9 %shard_map.56.refs_3_ = s16[64,2,1280]{2,1,0:T(2,128)(2,1)S(1)} custom-call(s32[1]{0:T(128)} %bitcast.grp, s32[64]{0:T(128)S(1)} %copy-done.3, bf16[288,5625]{1,0:T(8,128)(2,1)S(1)} %compare_select_fusion.rows, bf16[64,5625]{1,0:T(8,128)(2,1)S(1)} %bitcast.6, bf16[64,5625]{1,0:T(8,128)(2,1)S(1)} %collective-permute-done.4.refs_1_, ...), custom_call_target="tpu_custom_call" | custom-call | flops 2488320000 | bytes 5400000 | tf_op jit(solution)/shard_map/pallas_call | solution.py:145
  27.6 0.0 collective-permute-done.3.refs_0_
  27.7 1.9 %collective-permute-start.5 = (bf16[64,5625]{1,0:T(8,128)(2,1)S(1)}, bf16[64,5625]{1,0:T(8,128)(2,1)S(1)}, u32[]{:S(2)}, u32[]{:S(2)}) collective-permute-start(bf16[64,5625]{1,0:T(8,128)(2,1)S(1)} %collective-permute-done.refs_2_), channel_id=1, source_target_pairs={{0,64},{64,0},{128,192},{192,128},{256,320},{320,256},{384,448},{4... | collective-permute-start | bytes 2160008 | tf_op jit(solution)/shard_map/ppermute | solution.py:71
  29.6 2.4 %collective-permute-start.6 = (bf16[64,5625]{1,0:T(8,128)(2,1)S(1)}, bf16[64,5625]{1,0:T(8,128)(2,1)S(1)}, u32[]{:S(2)}, u32[]{:S(2)}) collective-permute-start(bf16[64,5625]{1,0:T(8,128)(2,1)S(1)} %collective-permute-done.3.refs_0_), channel_id=1, source_target_pairs={{0,64},{64,0},{128,192},{192,128},{256,320},{320,256},{384,448},{4... | collective-permute-start | bytes 2160008 | tf_op jit(solution)/shard_map/ppermute | solution.py:71
  32.0 0.2 collective-permute-done.1.refs_0_
  32.2 1.9 %collective-permute-start.2 = (bf16[64,5625]{1,0:T(8,128)(2,1)S(1)}, bf16[64,5625]{1,0:T(8,128)(2,1)S(1)}, u32[]{:S(2)}, u32[]{:S(2)}) collective-permute-start(bf16[64,5625]{1,0:T(8,128)(2,1)S(1)} %collective-permute-done.1.refs_0_), channel_id=1, source_target_pairs={{0,64},{64,0},{128,192},{192,128},{256,320},{320,256},{384,448},{4... | collective-permute-start | bytes 2160008 | tf_op jit(solution)/shard_map/ppermute | solution.py:71
  34.1 0.0 collective-permute-done.5.refs_1_
  34.1 0.0 collective-permute-done.6.refs_2_
  34.2 1.9 %shard_map.57.refs_2_ = s16[64,2,1280]{2,1,0:T(2,128)(2,1)S(1)} custom-call(s32[1]{0:T(128)} %bitcast.grp, s32[64]{0:T(128)S(1)} %copy-done.3, bf16[288,5625]{1,0:T(8,128)(2,1)S(1)} %compare_select_fusion.rows, bf16[64,5625]{1,0:T(8,128)(2,1)S(1)} %collective-permute-done.3.refs_0_, ...), custom_call_target="tpu_custom_call", output_to_operand_aliasing={{}: (6, {})} | custom-call | flops 2488320000 | bytes 5400000 | tf_op jit(solution)/shard_map/pallas_call | solution.py:145
  36.1 0.2 collective-permute-done.2.refs_1_
  36.3 1.8 %shard_map.58 = s16[64,2,1280]{2,1,0:T(2,128)(2,1)S(1)} custom-call(s32[1]{0:T(128)} %bitcast.grp, s32[64]{0:T(128)S(1)} %copy-done.3, bf16[288,5625]{1,0:T(8,128)(2,1)S(1)} %compare_select_fusion.rows, bf16[64,5625]{1,0:T(8,128)(2,1)S(1)} %collective-permute-done.1.refs_0_, ...), custom_call_target="tpu_custom_call", output_to_operand_aliasing={{}: (5, {})} | custom-call | flops 1658880000 | bytes 4680000 | tf_op jit(solution)/shard_map/pallas_call | solution.py:145
  38.1 29.1 %all_to_all.5.received = s16[64,2,1280]{2,1,0:T(2,128)(2,1)S(1)} all-to-all(s16[64,2,1280]{2,1,0:T(2,128)(2,1)S(1)} %shard_map.58), channel_id=1, replica_groups={{0,25,50,11,36,61,22,47,8,33,58,19,44,5,30,55,16,41,2,27,52,13,38,63,24..., dimensions={0} | all-to-all | bytes 655360 | tf_op jit(solution)/shard_map/all_to_all | solution.py:211
  67.3 0.8 %shard_map.59 = f32[8,288]{1,0:T(8,128)} custom-call(s16[64,2,1280]{2,1,0:T(2,128)(2,1)S(1)} %all_to_all.5.received), custom_call_target="tpu_custom_call" | custom-call | tf_op jit(solution)/shard_map/pallas_call | solution.py:179
  (4 shorter events, 0.0 us)
Async XLA Ops:
  0.0 14.7 %collective-permute-start = (bf16[64,5625]{1,0:T(8,128)(2,1)}, bf16[64,5625]{1,0:T(8,128)(2,1)S(1)}, u32[]{:S(2)}, u32[]{:S(2)}) collective-permute-start(bf16[64,5625]{1,0:T(8,128)(2,1)} %bitcast.3), channel_id=1, source_target_pairs={{0,128},{64,448},{128,0},{192,320},{256,384},{320,192},{384,256},{... | collective-permute-start | bytes 2160008 | tf_op jit(solution)/shard_map/ppermute | solution.py:67
  2.8 0.7 %copy-start = (s32[600]{0:T(1024)S(1)}, s32[600]{0:T(1024)}, u32[]{:S(2)}) copy-start(s32[600]{0:T(1024)} %refs_0_.1) | copy-start | bytes 7204
  3.5 0.7 %copy-start.1 = (s32[288]{0:T(512)S(1)}, s32[288]{0:T(512)}, u32[]{:S(2)}) copy-start(s32[288]{0:T(512)} %refs_1_.1) | copy-start | bytes 3460
  4.9 20.8 %collective-permute-start.4 = (bf16[64,5625]{1,0:T(8,128)(2,1)}, bf16[64,5625]{1,0:T(8,128)(2,1)S(1)}, u32[]{:S(2)}, u32[]{:S(2)}) collective-permute-start(bf16[64,5625]{1,0:T(8,128)(2,1)} %bitcast.4), channel_id=1, source_target_pairs={{0,64},{64,0},{128,192},{192,128},{256,320},{320,256},{384,448},{4... | collective-permute-start | bytes 2160008 | tf_op jit(solution)/shard_map/ppermute | solution.py:71
  6.8 20.8 %collective-permute-start.3 = (bf16[64,5625]{1,0:T(8,128)(2,1)}, bf16[64,5625]{1,0:T(8,128)(2,1)S(1)}, u32[]{:S(2)}, u32[]{:S(2)}) collective-permute-start(bf16[64,5625]{1,0:T(8,128)(2,1)} %bitcast.5), channel_id=1, source_target_pairs={{0,384},{64,192},{128,256},{192,64},{256,128},{320,448},{384,0},{4... | collective-permute-start | bytes 2160008 | tf_op jit(solution)/shard_map/ppermute | solution.py:67
  13.8 11.9 %copy-start.2 = (bf16[5625,64]{0,1:T(8,128)(2,1)S(1)}, bf16[5625,64]{0,1:T(8,128)(2,1)}, u32[]{:S(2)}) copy-start(bf16[5625,64]{0,1:T(8,128)(2,1)} %param.5) | copy-start | bytes 2160004
  13.8 11.9 %copy-start.3 = (s32[64]{0:T(128)S(1)}, s32[64]{0:T(128)}, u32[]{:S(2)}) copy-start(s32[64]{0:T(128)} %slot_pair.5) | copy-start | bytes 772
  14.7 17.5 %collective-permute-start.1 = (bf16[64,5625]{1,0:T(8,128)(2,1)S(1)}, bf16[64,5625]{1,0:T(8,128)(2,1)S(1)}, u32[]{:S(2)}, u32[]{:S(2)}) collective-permute-start(bf16[64,5625]{1,0:T(8,128)(2,1)S(1)} %collective-permute-done.refs_2_), channel_id=1, source_target_pairs={{0,384},{64,192},{128,256},{192,64},{256,128},{320,448},{384,0},{4... | collective-permute-start | bytes 2160008 | tf_op jit(solution)/shard_map/ppermute | solution.py:67
  27.7 6.5 %collective-permute-start.5 = (bf16[64,5625]{1,0:T(8,128)(2,1)S(1)}, bf16[64,5625]{1,0:T(8,128)(2,1)S(1)}, u32[]{:S(2)}, u32[]{:S(2)}) collective-permute-start(bf16[64,5625]{1,0:T(8,128)(2,1)S(1)} %collective-permute-done.refs_2_), channel_id=1, source_target_pairs={{0,64},{64,0},{128,192},{192,128},{256,320},{320,256},{384,448},{4... | collective-permute-start | bytes 2160008 | tf_op jit(solution)/shard_map/ppermute | solution.py:71
  29.6 4.6 %collective-permute-start.6 = (bf16[64,5625]{1,0:T(8,128)(2,1)S(1)}, bf16[64,5625]{1,0:T(8,128)(2,1)S(1)}, u32[]{:S(2)}, u32[]{:S(2)}) collective-permute-start(bf16[64,5625]{1,0:T(8,128)(2,1)S(1)} %collective-permute-done.3.refs_0_), channel_id=1, source_target_pairs={{0,64},{64,0},{128,192},{192,128},{256,320},{320,256},{384,448},{4... | collective-permute-start | bytes 2160008 | tf_op jit(solution)/shard_map/ppermute | solution.py:71
  32.2 4.1 %collective-permute-start.2 = (bf16[64,5625]{1,0:T(8,128)(2,1)S(1)}, bf16[64,5625]{1,0:T(8,128)(2,1)S(1)}, u32[]{:S(2)}, u32[]{:S(2)}) collective-permute-start(bf16[64,5625]{1,0:T(8,128)(2,1)S(1)} %collective-permute-done.1.refs_0_), channel_id=1, source_target_pairs={{0,64},{64,0},{128,192},{192,128},{256,320},{320,256},{384,448},{4... | collective-permute-start | bytes 2160008 | tf_op jit(solution)/shard_map/ppermute | solution.py:71

commit v7 on v6

--- a/solution.py
+++ b/solution.py
@@ -16,7 +16,7 @@
 TAIL = 32
 STEPS = 32000.0
 PAIRS = 64
-STRIDE = 25
+STRIDE = 41
 PLACE = pow(STRIDE, -1, PAIRS)
 SMALLEST = 1e-30
 VMEM_LIMIT = 10 << 20
@@ -59,7 +59,7 @@
 
 
 def neighbour(x, c):
-    return (N_X - 1 - x) * c + (x + 1 - 2 * (x % 2)) * (1 - c)
+    return (N_X - 1 - x) * (1 - c) + (x + 1 - 2 * (x % 2)) * c
 
 
 def other_chip(value, link):

time: 69.2 us -> 68.6 us (level)
  waiting for transfers between devices: 1.3 us -> 8.22 us
  starting transfers between devices: 26.1 us -> 20.3 us
  blocking collectives: 29.1 us -> 28 us
    ppermute x3, waiting for transfers between devices: 1.09 us -> 8.21 us  [other_chip(): return lax.ppermute(value, 'grp', pairs)]
    ppermute x3, starting transfers between devices: 18 us -> 11.6 us  [other_chip(): return lax.ppermute(value, 'grp', pairs)]
    all_to_all x1, blocking collectives: 29.1 us -> 28 us  [on_device(): lax.all_to_all(ordered, 'ef', 0, 0, tiled=True, axis_index_groups=members)]
  transfers between devices with their start and end apart: 7 -> 7, of which waited for: 3 -> 2; matrix products, arithmetic and copies ran while one was open for 5% -> 5% of each run, Pallas kernels for 6% -> 6%
where the time goes in v7:
time: 68.6 us; the launch traced here: 68 us
  blocking collectives  28 us (41%)
  starting transfers between devices  20.3 us (30%)
  waiting for transfers between devices  8.22 us (12%)
  Pallas kernels  6.48 us (9%)
  other arithmetic  3.2 us (5%)
  local copies, waits for them, and re-layouts  1.62 us (2%)
    all_to_all x1, blocking collectives, on_device(): lax.all_to_all(ordered, 'ef', 0, 0, tiled=True, axis_index_groups=members)  28 us
    ppermute x3, starting transfers between devices, other_chip(): return lax.ppermute(value, 'grp', pairs)  11.6 us
    ppermute x4, starting transfers between devices, other_core(): return lax.ppermute(value, 'grp', [(g, g ^ 1) for g in range(2 * N_X)])  8.71 us
    ppermute x3, waiting for transfers between devices, other_chip(): return lax.ppermute(value, 'grp', pairs)  8.21 us
    pallas_call x3, Pallas kernels, slot_products(): pl.pallas_call(functools.partial(product_kernel, part), out_shape=jax.Sha...  5.69 us
    select_n x1, other arithmetic, on_device(): jnp.where(row_sym[:, None] == col_sym[None, :], ladder, jnp.zeros((), lad...  2.72 us
    unnamed x8, local copies, waits for them, and re-layouts  1.37 us
  transfers between devices with their start and end apart: 7, of which 2 were waited for; matrix products, arithmetic and copies ran while one was open for 5% of the time, Pallas kernels for 6%

profile of v7, /device:TPU:6, one launch (start us, length us, event | category | flops | bytes accessed | tf_op | source)
XLA Modules:
  0.0 68.0 jit_solution(10080409573706655776)
XLA Ops:
  0.0 7.8 %collective-permute-start = (bf16[64,5625]{1,0:T(8,128)(2,1)}, bf16[64,5625]{1,0:T(8,128)(2,1)S(1)}, u32[]{:S(2)}, u32[]{:S(2)}) collective-permute-start(bf16[64,5625]{1,0:T(8,128)(2,1)} %bitcast.3), channel_id=1, source_target_pairs={{0,384},{64,192},{128,256},{192,64},{256,128},{320,448},{384,0},{4... | collective-permute-start | bytes 2160008 | tf_op jit(solution)/shard_map/ppermute | solution.py:67
  7.8 0.0 copy-start
  7.8 0.7 copy-done
  8.5 0.7 copy-done.1
  9.2 0.1 pad_dynamic-slice_fusion
  9.2 0.1 broadcast_xor_fusion
  9.3 0.1 xor.24
  9.4 0.1 dynamic_slice.7
  9.5 0.4 select_reduce_fusion
  9.9 1.9 %collective-permute-start.4 = (bf16[64,5625]{1,0:T(8,128)(2,1)}, bf16[64,5625]{1,0:T(8,128)(2,1)S(1)}, u32[]{:S(2)}, u32[]{:S(2)}) collective-permute-start(bf16[64,5625]{1,0:T(8,128)(2,1)} %bitcast.4), channel_id=1, source_target_pairs={{0,64},{64,0},{128,192},{192,128},{256,320},{320,256},{384,448},{4... | collective-permute-start | bytes 2160008 | tf_op jit(solution)/shard_map/ppermute | solution.py:71
  11.8 1.9 %collective-permute-start.3 = (bf16[64,5625]{1,0:T(8,128)(2,1)}, bf16[64,5625]{1,0:T(8,128)(2,1)S(1)}, u32[]{:S(2)}, u32[]{:S(2)}) collective-permute-start(bf16[64,5625]{1,0:T(8,128)(2,1)} %bitcast.5), channel_id=1, source_target_pairs={{0,128},{64,448},{128,0},{192,320},{256,384},{320,192},{384,256},{... | collective-permute-start | bytes 2160008 | tf_op jit(solution)/shard_map/ppermute | solution.py:67
  13.8 0.0 copy-start.2
  13.8 0.0 copy-start.3
  13.8 4.9 %collective-permute-done.refs_2_ = bf16[64,5625]{1,0:T(8,128)(2,1)S(1)} collective-permute-done((bf16[64,5625]{1,0:T(8,128)(2,1)}, bf16[64,5625]{1,0:T(8,128)(2,1)S(1)}, u32[]{:S(2)}, u32[]{:S(2)}) %collective-permute-start) | collective-permute-done | bytes 720032 | tf_op jit(solution)/shard_map/ppermute | solution.py:67
  18.7 1.9 %collective-permute-start.1 = (bf16[64,5625]{1,0:T(8,128)(2,1)S(1)}, bf16[64,5625]{1,0:T(8,128)(2,1)S(1)}, u32[]{:S(2)}, u32[]{:S(2)}) collective-permute-start(bf16[64,5625]{1,0:T(8,128)(2,1)S(1)} %collective-permute-done.refs_2_), channel_id=1, source_target_pairs={{0,128},{64,448},{128,0},{192,320},{256,384},{320,192},{384,256},{... | collective-permute-start | bytes 2160008 | tf_op jit(solution)/shard_map/ppermute | solution.py:67
  20.6 2.7 %compare_select_fusion.rows = bf16[288,5625]{1,0:T(8,128)(2,1)S(1)} fusion(bf16[288,5625]{1,0:T(8,128)(2,1)} %param.6, s32[5625]{0:T(1024)S(1)} %dynamic_slice.7, s32[288]{0:T(512)S(1)} %xor.20), kind=kLoop, calls=%fused_computation | loop fusion | flops 3240000 | bytes 6503652 | tf_op jit(solution)/shard_map/jit(_where)/select_n | solution.py:202
  23.3 0.0 collective-permute-done.4.refs_1_
  23.3 0.0 copy-done.2
  23.3 0.0 copy-done.3
  23.4 1.9 %shard_map.56.refs_3_ = s16[64,2,1280]{2,1,0:T(2,128)(2,1)S(1)} custom-call(s32[1]{0:T(128)} %bitcast.grp, s32[64]{0:T(128)S(1)} %copy-done.3, bf16[288,5625]{1,0:T(8,128)(2,1)S(1)} %compare_select_fusion.rows, bf16[64,5625]{1,0:T(8,128)(2,1)S(1)} %bitcast.6, bf16[64,5625]{1,0:T(8,128)(2,1)S(1)} %collective-permute-done.4.refs_1_, ...), custom_call_target="tpu_custom_call" | custom-call | flops 2488320000 | bytes 5400000 | tf_op jit(solution)/shard_map/pallas_call | solution.py:145
  25.3 0.0 collective-permute-done.3.refs_0_
  25.3 2.4 %collective-permute-start.5 = (bf16[64,5625]{1,0:T(8,128)(2,1)S(1)}, bf16[64,5625]{1,0:T(8,128)(2,1)S(1)}, u32[]{:S(2)}, u32[]{:S(2)}) collective-permute-start(bf16[64,5625]{1,0:T(8,128)(2,1)S(1)} %collective-permute-done.refs_2_), channel_id=1, source_target_pairs={{0,64},{64,0},{128,192},{192,128},{256,320},{320,256},{384,448},{4... | collective-permute-start | bytes 2160008 | tf_op jit(solution)/shard_map/ppermute | solution.py:71
  27.7 1.9 %collective-permute-start.6 = (bf16[64,5625]{1,0:T(8,128)(2,1)S(1)}, bf16[64,5625]{1,0:T(8,128)(2,1)S(1)}, u32[]{:S(2)}, u32[]{:S(2)}) collective-permute-start(bf16[64,5625]{1,0:T(8,128)(2,1)S(1)} %collective-permute-done.3.refs_0_), channel_id=1, source_target_pairs={{0,64},{64,0},{128,192},{192,128},{256,320},{320,256},{384,448},{4... | collective-permute-start | bytes 2160008 | tf_op jit(solution)/shard_map/ppermute | solution.py:71
  29.6 3.3 %collective-permute-done.1.refs_0_ = bf16[64,5625]{1,0:T(8,128)(2,1)S(1)} collective-permute-done((bf16[64,5625]{1,0:T(8,128)(2,1)S(1)}, bf16[64,5625]{1,0:T(8,128)(2,1)S(1)}, u32[]{:S(2)}, u32[]{:S(2)}) %collective-permute-start.1) | collective-permute-done | bytes 720032 | tf_op jit(solution)/shard_map/ppermute | solution.py:67
  33.0 2.5 %collective-permute-start.2 = (bf16[64,5625]{1,0:T(8,128)(2,1)S(1)}, bf16[64,5625]{1,0:T(8,128)(2,1)S(1)}, u32[]{:S(2)}, u32[]{:S(2)}) collective-permute-start(bf16[64,5625]{1,0:T(8,128)(2,1)S(1)} %collective-permute-done.1.refs_0_), channel_id=1, source_target_pairs={{0,64},{64,0},{128,192},{192,128},{256,320},{320,256},{384,448},{4... | collective-permute-start | bytes 2160008 | tf_op jit(solution)/shard_map/ppermute | solution.py:71
  35.4 0.0 collective-permute-done.5.refs_1_
  35.4 0.0 collective-permute-done.6.refs_2_
  35.5 1.9 %shard_map.57.refs_2_ = s16[64,2,1280]{2,1,0:T(2,128)(2,1)S(1)} custom-call(s32[1]{0:T(128)} %bitcast.grp, s32[64]{0:T(128)S(1)} %copy-done.3, bf16[288,5625]{1,0:T(8,128)(2,1)S(1)} %compare_select_fusion.rows, bf16[64,5625]{1,0:T(8,128)(2,1)S(1)} %collective-permute-done.3.refs_0_, ...), custom_call_target="tpu_custom_call", output_to_operand_aliasing={{}: (6, {})} | custom-call | flops 2488320000 | bytes 5400000 | tf_op jit(solution)/shard_map/pallas_call | solution.py:145
  37.4 0.0 collective-permute-done.2.refs_1_
  37.4 1.9 %shard_map.58 = s16[64,2,1280]{2,1,0:T(2,128)(2,1)S(1)} custom-call(s32[1]{0:T(128)} %bitcast.grp, s32[64]{0:T(128)S(1)} %copy-done.3, bf16[288,5625]{1,0:T(8,128)(2,1)S(1)} %compare_select_fusion.rows, bf16[64,5625]{1,0:T(8,128)(2,1)S(1)} %collective-permute-done.1.refs_0_, ...), custom_call_target="tpu_custom_call", output_to_operand_aliasing={{}: (5, {})} | custom-call | flops 1658880000 | bytes 4680000 | tf_op jit(solution)/shard_map/pallas_call | solution.py:145
  39.2 28.0 %all_to_all.5.received = s16[64,2,1280]{2,1,0:T(2,128)(2,1)S(1)} all-to-all(s16[64,2,1280]{2,1,0:T(2,128)(2,1)S(1)} %shard_map.58), channel_id=1, replica_groups={{0,41,18,59,36,13,54,31,8,49,26,3,44,21,62,39,16,57,34,11,52,29,6,47,24..., dimensions={0} | all-to-all | bytes 655360 | tf_op jit(solution)/shard_map/all_to_all | solution.py:211
  67.2 0.8 %shard_map.59 = f32[8,288]{1,0:T(8,128)} custom-call(s16[64,2,1280]{2,1,0:T(2,128)(2,1)S(1)} %all_to_all.5.received), custom_call_target="tpu_custom_call" | custom-call | tf_op jit(solution)/shard_map/pallas_call | solution.py:179
  (4 shorter events, 0.0 us)
Async XLA Ops:
  0.0 18.7 %collective-permute-start = (bf16[64,5625]{1,0:T(8,128)(2,1)}, bf16[64,5625]{1,0:T(8,128)(2,1)S(1)}, u32[]{:S(2)}, u32[]{:S(2)}) collective-permute-start(bf16[64,5625]{1,0:T(8,128)(2,1)} %bitcast.3), channel_id=1, source_target_pairs={{0,384},{64,192},{128,256},{192,64},{256,128},{320,448},{384,0},{4... | collective-permute-start | bytes 2160008 | tf_op jit(solution)/shard_map/ppermute | solution.py:67
  7.8 0.7 %copy-start = (s32[600]{0:T(1024)S(1)}, s32[600]{0:T(1024)}, u32[]{:S(2)}) copy-start(s32[600]{0:T(1024)} %refs_0_.1) | copy-start | bytes 7204
  8.5 0.7 %copy-start.1 = (s32[288]{0:T(512)S(1)}, s32[288]{0:T(512)}, u32[]{:S(2)}) copy-start(s32[288]{0:T(512)} %refs_1_.1) | copy-start | bytes 3460
  9.9 13.4 %collective-permute-start.4 = (bf16[64,5625]{1,0:T(8,128)(2,1)}, bf16[64,5625]{1,0:T(8,128)(2,1)S(1)}, u32[]{:S(2)}, u32[]{:S(2)}) collective-permute-start(bf16[64,5625]{1,0:T(8,128)(2,1)} %bitcast.4), channel_id=1, source_target_pairs={{0,64},{64,0},{128,192},{192,128},{256,320},{320,256},{384,448},{4... | collective-permute-start | bytes 2160008 | tf_op jit(solution)/shard_map/ppermute | solution.py:71
  11.8 13.4 %collective-permute-start.3 = (bf16[64,5625]{1,0:T(8,128)(2,1)}, bf16[64,5625]{1,0:T(8,128)(2,1)S(1)}, u32[]{:S(2)}, u32[]{:S(2)}) collective-permute-start(bf16[64,5625]{1,0:T(8,128)(2,1)} %bitcast.5), channel_id=1, source_target_pairs={{0,128},{64,448},{128,0},{192,320},{256,384},{320,192},{384,256},{... | collective-permute-start | bytes 2160008 | tf_op jit(solution)/shard_map/ppermute | solution.py:67
  13.8 9.6 %copy-start.2 = (bf16[5625,64]{0,1:T(8,128)(2,1)S(1)}, bf16[5625,64]{0,1:T(8,128)(2,1)}, u32[]{:S(2)}) copy-start(bf16[5625,64]{0,1:T(8,128)(2,1)} %param.5) | copy-start | bytes 2160004
  13.8 9.6 %copy-start.3 = (s32[64]{0:T(128)S(1)}, s32[64]{0:T(128)}, u32[]{:S(2)}) copy-start(s32[64]{0:T(128)} %slot_pair.5) | copy-start | bytes 772
  18.7 14.3 %collective-permute-start.1 = (bf16[64,5625]{1,0:T(8,128)(2,1)S(1)}, bf16[64,5625]{1,0:T(8,128)(2,1)S(1)}, u32[]{:S(2)}, u32[]{:S(2)}) collective-permute-start(bf16[64,5625]{1,0:T(8,128)(2,1)S(1)} %collective-permute-done.refs_2_), channel_id=1, source_target_pairs={{0,128},{64,448},{128,0},{192,320},{256,384},{320,192},{384,256},{... | collective-permute-start | bytes 2160008 | tf_op jit(solution)/shard_map/ppermute | solution.py:67
  25.3 10.1 %collective-permute-start.5 = (bf16[64,5625]{1,0:T(8,128)(2,1)S(1)}, bf16[64,5625]{1,0:T(8,128)(2,1)S(1)}, u32[]{:S(2)}, u32[]{:S(2)}) collective-permute-start(bf16[64,5625]{1,0:T(8,128)(2,1)S(1)} %collective-permute-done.refs_2_), channel_id=1, source_target_pairs={{0,64},{64,0},{128,192},{192,128},{256,320},{320,256},{384,448},{4... | collective-permute-start | bytes 2160008 | tf_op jit(solution)/shard_map/ppermute | solution.py:71
  27.7 7.7 %collective-permute-start.6 = (bf16[64,5625]{1,0:T(8,128)(2,1)S(1)}, bf16[64,5625]{1,0:T(8,128)(2,1)S(1)}, u32[]{:S(2)}, u32[]{:S(2)}) collective-permute-start(bf16[64,5625]{1,0:T(8,128)(2,1)S(1)} %collective-permute-done.3.refs_0_), channel_id=1, source_target_pairs={{0,64},{64,0},{128,192},{192,128},{256,320},{320,256},{384,448},{4... | collective-permute-start | bytes 2160008 | tf_op jit(solution)/shard_map/ppermute | solution.py:71
  33.0 4.4 %collective-permute-start.2 = (bf16[64,5625]{1,0:T(8,128)(2,1)S(1)}, bf16[64,5625]{1,0:T(8,128)(2,1)S(1)}, u32[]{:S(2)}, u32[]{:S(2)}) collective-permute-start(bf16[64,5625]{1,0:T(8,128)(2,1)S(1)} %collective-permute-done.1.refs_0_), channel_id=1, source_target_pairs={{0,64},{64,0},{128,192},{192,128},{256,320},{320,256},{384,448},{4... | collective-permute-start | bytes 2160008 | tf_op jit(solution)/shard_map/ppermute | solution.py:71

commit v8 on v7

--- a/solution.py
+++ b/solution.py
@@ -14,11 +14,9 @@
 CHUNK = 1024
 LANES = 128
 TAIL = 32
-STEPS = 32000.0
 PAIRS = 64
 STRIDE = 41
 PLACE = pow(STRIDE, -1, PAIRS)
-SMALLEST = 1e-30
 VMEM_LIMIT = 10 << 20
 
 VMEM = pl.BlockSpec(memory_space=pltpu.VMEM)
@@ -84,7 +82,7 @@
     return total.T
 
 
-def pack(out, pair, block, exponent):
+def pack(out, pair, block):
     lane = lax.broadcasted_iota(jnp.int32, (2, LANES), 1)
     tail = block[:2, 2 * LANES :]
     for j in range(1, ROOTS // 2):
@@ -92,23 +90,15 @@
         tail = jnp.where(lane >= j * TAIL, piece, tail)
     pieces = [block[2 * j : 2 * j + 2, :LANES] for j in range(ROOTS // 2)]
     pieces += [block[2 * j : 2 * j + 2, LANES : 2 * LANES] for j in range(ROOTS // 2)]
-    out[pair] = jnp.concatenate(pieces + [tail, exponent], axis=1).astype(out.dtype)
-
-
-def store_slots(grp, slot_pair, owners, held, steps, exponents, out):
-    count = held.shape[0] // ROOTS
-    values = held[...].reshape(count, ROOTS, held.shape[1])
-    largest = jnp.max(jnp.max(jnp.abs(values), axis=1, keepdims=True), axis=2, keepdims=True)
-    exponent = jnp.floor(jnp.log2(jnp.maximum(largest, SMALLEST))) + 1.0
-    scale = jnp.exp2(-exponent) * STEPS
-    steps[...] = jnp.round(values * scale).astype(jnp.int32)
-    exponents[...] = jnp.broadcast_to(exponent, exponents.shape).astype(jnp.int32)
+    out[pair] = jnp.concatenate(pieces + [tail], axis=1)
+
+
+def store_slots(grp, slot_pair, owners, held, out):
     for block, (chip, core) in enumerate(owners):
         group = lax.rem(chip, N_X) * 2 + core
         for slot in range(GROUP_SLOTS):
             pair = lax.rem(slot_pair[group * GROUP_SLOTS + slot] * PLACE, PAIRS)
-            index = block * GROUP_SLOTS + slot
-            pack(out, pair, steps[index], exponents[index])
+            pack(out, pair, held[pl.ds((block * GROUP_SLOTS + slot) * ROOTS, ROOTS), :])
 
 
 def owners_of(grp, part):
@@ -123,11 +113,11 @@
 
 def product_kernel(part, grp, slot_pair, rows, *refs):
     owners = owners_of(grp, part)
-    out, held, steps, exponents = refs[-4:]
+    out, held = refs[-2:]
     count = rows.shape[0]
     held[:, 2 * LANES :] = jnp.zeros((held.shape[0], LANES), held.dtype)
     held[:, :count] = product(refs[: len(owners)], rows)
-    store_slots(grp, slot_pair, owners, held, steps, exponents, out)
+    store_slots(grp, slot_pair, owners, held, out)
 
 
 def estimate(columns, rows):
@@ -144,14 +134,10 @@
     before = [] if ordered is None else [ordered]
     return pl.pallas_call(
         functools.partial(product_kernel, part),
-        out_shape=jax.ShapeDtypeStruct((slot_pair.shape[0], 2, 10 * LANES), jnp.int16),
+        out_shape=jax.ShapeDtypeStruct((slot_pair.shape[0], 2, 9 * LANES), jnp.float32),
         in_specs=[SMEM, SMEM, VMEM] + [VMEM] * len(columns) + [VMEM] * len(before),
         out_specs=VMEM,
-        scratch_shapes=[
-            pltpu.VMEM((count, 3 * LANES), jnp.float32),
-            pltpu.VMEM((count // ROOTS, ROOTS, 3 * LANES), jnp.int32),
-            pltpu.VMEM((count // ROOTS, 2, LANES), jnp.int32),
-        ],
+        scratch_shapes=[pltpu.VMEM((count, 3 * LANES), jnp.float32)],
         input_output_aliases={3 + len(columns): 0} if before else {},
         compiler_params=pltpu.CompilerParams(vmem_limit_bytes=VMEM_LIMIT),
         cost_estimate=estimate(columns, rows),
@@ -159,13 +145,9 @@
 
 
 def total_kernel(received, out):
-    width = 9 * LANES
-    total = jnp.zeros((2, width), jnp.float32)
-    for sender in range(received.shape[0]):
-        exponent = received[sender, :, width:].astype(jnp.int32).astype(jnp.float32)
-        unit = jnp.concatenate([jnp.exp2(exponent) * (1.0 / STEPS)] * 9, axis=1)
-        steps = received[sender, :, :width].astype(jnp.int32).astype(jnp.float32)
-        total = total + steps * unit
+    total = received[0]
+    for sender in range(1, received.shape[0]):
+        total = total + received[sender]
     for j in range(ROOTS // 2):
         two = slice(2 * j, 2 * j + 2)
         out[two, :LANES] = total[:, j * LANES : (j + 1) * LANES]

time: 68.6 us -> 74.1 us (1.080)
  blocking collectives: 28 us -> 33.4 us
    all_to_all x1, blocking collectives: 28 us -> 33.4 us  [on_device(): lax.all_to_all(ordered, 'ef', 0, 0, tiled=True, axis_index_groups=members)]
  transfers between devices with their start and end apart: 7 -> 7, of which waited for: 2 -> 3; matrix products, arithmetic and copies ran while one was open for 5% -> 5% of each run, Pallas kernels for 6% -> 5%
where the time goes in v8:
time: 74.1 us; the launch traced here: 73.2 us
  blocking collectives  33.4 us (45%)
  starting transfers between devices  20.3 us (27%)
  waiting for transfers between devices  8.3 us (11%)
  Pallas kernels  6.08 us (8%)
  other arithmetic  3.2 us (4%)
  local copies, waits for them, and re-layouts  1.62 us (2%)
    all_to_all x1, blocking collectives, on_device(): lax.all_to_all(ordered, 'ef', 0, 0, tiled=True, axis_index_groups=members)  33.4 us
    ppermute x3, starting transfers between devices, other_chip(): return lax.ppermute(value, 'grp', pairs)  11.6 us
    ppermute x4, starting transfers between devices, other_core(): return lax.ppermute(value, 'grp', [(g, g ^ 1) for g in range(2 * N_X)])  8.75 us
    ppermute x3, waiting for transfers between devices, other_chip(): return lax.ppermute(value, 'grp', pairs)  8.29 us
    pallas_call x3, Pallas kernels, slot_products(): pl.pallas_call(functools.partial(product_kernel, part), out_shape=jax.Sha...  5.34 us
    select_n x1, other arithmetic, on_device(): jnp.where(row_sym[:, None] == col_sym[None, :], ladder, jnp.zeros((), lad...  2.72 us
  transfers between devices with their start and end apart: 7, of which 3 were waited for; matrix products, arithmetic and copies ran while one was open for 5% of the time, Pallas kernels for 5%

profile of v8, /device:TPU:6, one launch (start us, length us, event | category | flops | bytes accessed | tf_op | source)
XLA Modules:
  0.0 73.2 jit_solution(15703422243763824476)
XLA Ops:
  0.0 7.8 %collective-permute-start = (bf16[64,5625]{1,0:T(8,128)(2,1)}, bf16[64,5625]{1,0:T(8,128)(2,1)S(1)}, u32[]{:S(2)}, u32[]{:S(2)}) collective-permute-start(bf16[64,5625]{1,0:T(8,128)(2,1)} %bitcast.3), channel_id=1, source_target_pairs={{0,384},{64,192},{128,256},{192,64},{256,128},{320,448},{384,0},{4... | collective-permute-start | bytes 2160008 | tf_op jit(solution)/shard_map/ppermute | solution.py:65
  7.8 0.0 copy-start
  7.8 0.7 copy-done
  8.5 0.7 copy-done.1
  9.2 0.1 pad_dynamic-slice_fusion
  9.2 0.1 broadcast_xor_fusion
  9.3 0.1 xor.24
  9.4 0.1 dynamic_slice.7
  9.5 0.4 select_reduce_fusion
  9.9 1.9 %collective-permute-start.4 = (bf16[64,5625]{1,0:T(8,128)(2,1)}, bf16[64,5625]{1,0:T(8,128)(2,1)S(1)}, u32[]{:S(2)}, u32[]{:S(2)}) collective-permute-start(bf16[64,5625]{1,0:T(8,128)(2,1)} %bitcast.4), channel_id=1, source_target_pairs={{0,64},{64,0},{128,192},{192,128},{256,320},{320,256},{384,448},{4... | collective-permute-start | bytes 2160008 | tf_op jit(solution)/shard_map/ppermute | solution.py:69
  11.8 1.9 %collective-permute-start.3 = (bf16[64,5625]{1,0:T(8,128)(2,1)}, bf16[64,5625]{1,0:T(8,128)(2,1)S(1)}, u32[]{:S(2)}, u32[]{:S(2)}) collective-permute-start(bf16[64,5625]{1,0:T(8,128)(2,1)} %bitcast.5), channel_id=1, source_target_pairs={{0,128},{64,448},{128,0},{192,320},{256,384},{320,192},{384,256},{... | collective-permute-start | bytes 2160008 | tf_op jit(solution)/shard_map/ppermute | solution.py:65
  13.8 0.0 copy-start.2
  13.8 0.0 copy-start.3
  13.8 4.9 %collective-permute-done.refs_2_ = bf16[64,5625]{1,0:T(8,128)(2,1)S(1)} collective-permute-done((bf16[64,5625]{1,0:T(8,128)(2,1)}, bf16[64,5625]{1,0:T(8,128)(2,1)S(1)}, u32[]{:S(2)}, u32[]{:S(2)}) %collective-permute-start) | collective-permute-done | bytes 720032 | tf_op jit(solution)/shard_map/ppermute | solution.py:65
  18.7 1.9 %collective-permute-start.1 = (bf16[64,5625]{1,0:T(8,128)(2,1)S(1)}, bf16[64,5625]{1,0:T(8,128)(2,1)S(1)}, u32[]{:S(2)}, u32[]{:S(2)}) collective-permute-start(bf16[64,5625]{1,0:T(8,128)(2,1)S(1)} %collective-permute-done.refs_2_), channel_id=1, source_target_pairs={{0,128},{64,448},{128,0},{192,320},{256,384},{320,192},{384,256},{... | collective-permute-start | bytes 2160008 | tf_op jit(solution)/shard_map/ppermute | solution.py:65
  20.6 2.7 %compare_select_fusion.rows = bf16[288,5625]{1,0:T(8,128)(2,1)S(1)} fusion(bf16[288,5625]{1,0:T(8,128)(2,1)} %param.6, s32[5625]{0:T(1024)S(1)} %dynamic_slice.7, s32[288]{0:T(512)S(1)} %xor.20), kind=kLoop, calls=%fused_computation | loop fusion | flops 3240000 | bytes 6503652 | tf_op jit(solution)/shard_map/jit(_where)/select_n | solution.py:184
  23.3 0.0 collective-permute-done.4.refs_1_
  23.3 0.0 copy-done.2
  23.3 0.0 copy-done.3
  23.4 1.8 %shard_map.56.refs_3_ = f32[64,2,1152]{2,1,0:T(2,128)S(1)} custom-call(s32[1]{0:T(128)} %bitcast.grp, s32[64]{0:T(128)S(1)} %copy-done.3, bf16[288,5625]{1,0:T(8,128)(2,1)S(1)} %compare_select_fusion.rows, bf16[64,5625]{1,0:T(8,128)(2,1)S(1)} %bitcast.6, bf16[64,5625]{1,0:T(8,128)(2,1)S(1)} %collective-permute-done.4.refs_1_, ...), custom_call_target="tpu_custom_call" | custom-call | flops 2488320000 | bytes 5400000 | tf_op jit(solution)/shard_map/pallas_call | solution.py:135
  25.2 0.1 collective-permute-done.3.refs_0_
  25.2 2.5 %collective-permute-start.5 = (bf16[64,5625]{1,0:T(8,128)(2,1)S(1)}, bf16[64,5625]{1,0:T(8,128)(2,1)S(1)}, u32[]{:S(2)}, u32[]{:S(2)}) collective-permute-start(bf16[64,5625]{1,0:T(8,128)(2,1)S(1)} %collective-permute-done.refs_2_), channel_id=1, source_target_pairs={{0,64},{64,0},{128,192},{192,128},{256,320},{320,256},{384,448},{4... | collective-permute-start | bytes 2160008 | tf_op jit(solution)/shard_map/ppermute | solution.py:69
  27.7 1.9 %collective-permute-start.6 = (bf16[64,5625]{1,0:T(8,128)(2,1)S(1)}, bf16[64,5625]{1,0:T(8,128)(2,1)S(1)}, u32[]{:S(2)}, u32[]{:S(2)}) collective-permute-start(bf16[64,5625]{1,0:T(8,128)(2,1)S(1)} %collective-permute-done.3.refs_0_), channel_id=1, source_target_pairs={{0,64},{64,0},{128,192},{192,128},{256,320},{320,256},{384,448},{4... | collective-permute-start | bytes 2160008 | tf_op jit(solution)/shard_map/ppermute | solution.py:69
  29.6 3.3 %collective-permute-done.1.refs_0_ = bf16[64,5625]{1,0:T(8,128)(2,1)S(1)} collective-permute-done((bf16[64,5625]{1,0:T(8,128)(2,1)S(1)}, bf16[64,5625]{1,0:T(8,128)(2,1)S(1)}, u32[]{:S(2)}, u32[]{:S(2)}) %collective-permute-start.1) | collective-permute-done | bytes 720032 | tf_op jit(solution)/shard_map/ppermute | solution.py:65
  33.0 2.5 %collective-permute-start.2 = (bf16[64,5625]{1,0:T(8,128)(2,1)S(1)}, bf16[64,5625]{1,0:T(8,128)(2,1)S(1)}, u32[]{:S(2)}, u32[]{:S(2)}) collective-permute-start(bf16[64,5625]{1,0:T(8,128)(2,1)S(1)} %collective-permute-done.1.refs_0_), channel_id=1, source_target_pairs={{0,64},{64,0},{128,192},{192,128},{256,320},{320,256},{384,448},{4... | collective-permute-start | bytes 2160008 | tf_op jit(solution)/shard_map/ppermute | solution.py:69
  35.4 0.0 collective-permute-done.5.refs_1_
  35.4 0.0 collective-permute-done.6.refs_2_
  35.5 1.8 %shard_map.57.refs_2_ = f32[64,2,1152]{2,1,0:T(2,128)S(1)} custom-call(s32[1]{0:T(128)} %bitcast.grp, s32[64]{0:T(128)S(1)} %copy-done.3, bf16[288,5625]{1,0:T(8,128)(2,1)S(1)} %compare_select_fusion.rows, bf16[64,5625]{1,0:T(8,128)(2,1)S(1)} %collective-permute-done.3.refs_0_, ...), custom_call_target="tpu_custom_call", output_to_operand_aliasing={{}: (6, {})} | custom-call | flops 2488320000 | bytes 5400000 | tf_op jit(solution)/shard_map/pallas_call | solution.py:135
  37.3 0.0 collective-permute-done.2.refs_1_
  37.3 1.7 %shard_map.58 = f32[64,2,1152]{2,1,0:T(2,128)S(1)} custom-call(s32[1]{0:T(128)} %bitcast.grp, s32[64]{0:T(128)S(1)} %copy-done.3, bf16[288,5625]{1,0:T(8,128)(2,1)S(1)} %compare_select_fusion.rows, bf16[64,5625]{1,0:T(8,128)(2,1)S(1)} %collective-permute-done.1.refs_0_, ...), custom_call_target="tpu_custom_call", output_to_operand_aliasing={{}: (5, {})} | custom-call | flops 1658880000 | bytes 4680000 | tf_op jit(solution)/shard_map/pallas_call | solution.py:135
  39.0 33.4 %all_to_all.5.received = f32[64,2,1152]{2,1,0:T(2,128)S(1)} all-to-all(f32[64,2,1152]{2,1,0:T(2,128)S(1)} %shard_map.58), channel_id=1, replica_groups={{0,41,18,59,36,13,54,31,8,49,26,3,44,21,62,39,16,57,34,11,52,29,6,47,24..., dimensions={0} | all-to-all | bytes 1179648 | tf_op jit(solution)/shard_map/all_to_all | solution.py:193
  72.5 0.7 %shard_map.59 = f32[8,288]{1,0:T(8,128)} custom-call(f32[64,2,1152]{2,1,0:T(2,128)S(1)} %all_to_all.5.received), custom_call_target="tpu_custom_call" | custom-call | tf_op jit(solution)/shard_map/pallas_call | solution.py:161
  (4 shorter events, 0.0 us)
Async XLA Ops:
  0.0 18.7 %collective-permute-start = (bf16[64,5625]{1,0:T(8,128)(2,1)}, bf16[64,5625]{1,0:T(8,128)(2,1)S(1)}, u32[]{:S(2)}, u32[]{:S(2)}) collective-permute-start(bf16[64,5625]{1,0:T(8,128)(2,1)} %bitcast.3), channel_id=1, source_target_pairs={{0,384},{64,192},{128,256},{192,64},{256,128},{320,448},{384,0},{4... | collective-permute-start | bytes 2160008 | tf_op jit(solution)/shard_map/ppermute | solution.py:65
  7.8 0.7 copy-start
  8.5 0.7 copy-start.1
  9.9 13.4 %collective-permute-start.4 = (bf16[64,5625]{1,0:T(8,128)(2,1)}, bf16[64,5625]{1,0:T(8,128)(2,1)S(1)}, u32[]{:S(2)}, u32[]{:S(2)}) collective-permute-start(bf16[64,5625]{1,0:T(8,128)(2,1)} %bitcast.4), channel_id=1, source_target_pairs={{0,64},{64,0},{128,192},{192,128},{256,320},{320,256},{384,448},{4... | collective-permute-start | bytes 2160008 | tf_op jit(solution)/shard_map/ppermute | solution.py:69
  11.8 13.4 %collective-permute-start.3 = (bf16[64,5625]{1,0:T(8,128)(2,1)}, bf16[64,5625]{1,0:T(8,128)(2,1)S(1)}, u32[]{:S(2)}, u32[]{:S(2)}) collective-permute-start(bf16[64,5625]{1,0:T(8,128)(2,1)} %bitcast.5), channel_id=1, source_target_pairs={{0,128},{64,448},{128,0},{192,320},{256,384},{320,192},{384,256},{... | collective-permute-start | bytes 2160008 | tf_op jit(solution)/shard_map/ppermute | solution.py:65
  13.8 9.6 %copy-start.2 = (bf16[5625,64]{0,1:T(8,128)(2,1)S(1)}, bf16[5625,64]{0,1:T(8,128)(2,1)}, u32[]{:S(2)}) copy-start(bf16[5625,64]{0,1:T(8,128)(2,1)} %param.5) | copy-start | bytes 2160004
  13.8 9.6 %copy-start.3 = (s32[64]{0:T(128)S(1)}, s32[64]{0:T(128)}, u32[]{:S(2)}) copy-start(s32[64]{0:T(128)} %slot_pair.5) | copy-start | bytes 772
  18.7 14.3 %collective-permute-start.1 = (bf16[64,5625]{1,0:T(8,128)(2,1)S(1)}, bf16[64,5625]{1,0:T(8,128)(2,1)S(1)}, u32[]{:S(2)}, u32[]{:S(2)}) collective-permute-start(bf16[64,5625]{1,0:T(8,128)(2,1)S(1)} %collective-permute-done.refs_2_), channel_id=1, source_target_pairs={{0,128},{64,448},{128,0},{192,320},{256,384},{320,192},{384,256},{... | collective-permute-start | bytes 2160008 | tf_op jit(solution)/shard_map/ppermute | solution.py:65
  25.2 10.2 %collective-permute-start.5 = (bf16[64,5625]{1,0:T(8,128)(2,1)S(1)}, bf16[64,5625]{1,0:T(8,128)(2,1)S(1)}, u32[]{:S(2)}, u32[]{:S(2)}) collective-permute-start(bf16[64,5625]{1,0:T(8,128)(2,1)S(1)} %collective-permute-done.refs_2_), channel_id=1, source_target_pairs={{0,64},{64,0},{128,192},{192,128},{256,320},{320,256},{384,448},{4... | collective-permute-start | bytes 2160008 | tf_op jit(solution)/shard_map/ppermute | solution.py:69
  27.7 7.7 %collective-permute-start.6 = (bf16[64,5625]{1,0:T(8,128)(2,1)S(1)}, bf16[64,5625]{1,0:T(8,128)(2,1)S(1)}, u32[]{:S(2)}, u32[]{:S(2)}) collective-permute-start(bf16[64,5625]{1,0:T(8,128)(2,1)S(1)} %collective-permute-done.3.refs_0_), channel_id=1, source_target_pairs={{0,64},{64,0},{128,192},{192,128},{256,320},{320,256},{384,448},{4... | collective-permute-start | bytes 2160008 | tf_op jit(solution)/shard_map/ppermute | solution.py:69
  33.0 4.3 %collective-permute-start.2 = (bf16[64,5625]{1,0:T(8,128)(2,1)S(1)}, bf16[64,5625]{1,0:T(8,128)(2,1)S(1)}, u32[]{:S(2)}, u32[]{:S(2)}) collective-permute-start(bf16[64,5625]{1,0:T(8,128)(2,1)S(1)} %collective-permute-done.1.refs_0_), channel_id=1, source_target_pairs={{0,64},{64,0},{128,192},{192,128},{256,320},{320,256},{384,448},{4... | collective-permute-start | bytes 2160008 | tf_op jit(solution)/shard_map/ppermute | solution.py:69

commit v9 on v7

--- a/solution.py
+++ b/solution.py
@@ -190,15 +190,15 @@
     own = amplitudes.T
     mine = other_chip(own, 0)
 
-    orbital_irrep, panel_rows = near_copies(orbital_irrep, panel_rows)
+    (orbital_irrep,) = near_copies(orbital_irrep)
     col_sym = column_symmetry(orbital_irrep, ladder.shape[1])
+    first, col_sym = lax.optimization_barrier((own, col_sym))
+    theirs, own_other = other_chip(first, 1), other_core(first)
+    mine, col_sym = lax.optimization_barrier((mine, col_sym))
+    far = other_chip(mine, 1)
     row_sym = jnp.bitwise_xor(
         lookup(panel_rows // V, orbital_irrep), lookup(panel_rows % V, orbital_irrep)
     )
-    first, row_sym, col_sym = lax.optimization_barrier((own, row_sym, col_sym))
-    theirs, own_other = other_chip(first, 1), other_core(first)
-    mine, row_sym, col_sym = lax.optimization_barrier((mine, row_sym, col_sym))
-    far = other_chip(mine, 1)
     masked = jnp.where(row_sym[:, None] == col_sym[None, :], ladder, jnp.zeros((), ladder.dtype))
     ordered = slot_products("first", grp, slot_pair, masked, (own, own_other, mine))
     mine, theirs, ordered = lax.optimization_barrier((mine, theirs, ordered))

time: 68.6 us -> 69.4 us (1.012)
  blocking collectives: 28 us -> 29.3 us
  other arithmetic: 3.2 us -> 3.9 us
    all_to_all x1, blocking collectives: 28 us -> 29.3 us  [on_device(): lax.all_to_all(ordered, 'ef', 0, 0, tiled=True, axis_index_groups=members)]
  transfers between devices with their start and end apart: 7 -> 7, of which waited for: 2 -> 3; matrix products, arithmetic and copies ran while one was open for 5% -> 6% of each run, Pallas kernels for 6% -> 6%
where the time goes in v9:
time: 69.4 us; the launch traced here: 69 us
  blocking collectives  29.3 us (42%)
  starting transfers between devices  19.7 us (28%)
  waiting for transfers between devices  8.42 us (12%)
  Pallas kernels  6.47 us (9%)
  other arithmetic  3.9 us (6%)
  local copies, waits for them, and re-layouts  0.94 us (1%)
    all_to_all x1, blocking collectives, on_device(): lax.all_to_all(ordered, 'ef', 0, 0, tiled=True, axis_index_groups=members)  29.3 us
    ppermute x3, starting transfers between devices, other_chip(): return lax.ppermute(value, 'grp', pairs)  11.6 us
    ppermute x3, waiting for transfers between devices, other_chip(): return lax.ppermute(value, 'grp', pairs)  8.2 us
    ppermute x4, starting transfers between devices, other_core(): return lax.ppermute(value, 'grp', [(g, g ^ 1) for g in range(2 * N_X)])  8.15 us
    pallas_call x3, Pallas kernels, slot_products(): pl.pallas_call(functools.partial(product_kernel, part), out_shape=jax.Sha...  5.68 us
    select_n x1, other arithmetic, on_device(): jnp.where(row_sym[:, None] == col_sym[None, :], ladder, jnp.zeros((), lad...  2.74 us
  transfers between devices with their start and end apart: 7, of which 3 were waited for; matrix products, arithmetic and copies ran while one was open for 6% of the time, Pallas kernels for 6%

profile of v9, /device:TPU:6, one launch (start us, length us, event | category | flops | bytes accessed | tf_op | source)
XLA Modules:
  0.0 69.0 jit_solution(12922065936529396997)
XLA Ops:
  0.0 7.8 %collective-permute-start = (bf16[64,5625]{1,0:T(8,128)(2,1)}, bf16[64,5625]{1,0:T(8,128)(2,1)S(1)}, u32[]{:S(2)}, u32[]{:S(2)}) collective-permute-start(bf16[64,5625]{1,0:T(8,128)(2,1)} %bitcast.3), channel_id=1, source_target_pairs={{0,384},{64,192},{128,256},{192,64},{256,128},{320,448},{384,0},{4... | collective-permute-start | bytes 2160008 | tf_op jit(solution)/shard_map/ppermute | solution.py:67
  7.8 0.0 copy-start
  7.8 0.7 copy-done
  8.5 0.1 pad_dynamic-slice_fusion
  8.6 0.1 broadcast_xor_fusion
  8.6 0.1 xor.28
  8.7 0.1 dynamic_slice.7
  8.8 1.9 %collective-permute-start.4 = (bf16[64,5625]{1,0:T(8,128)(2,1)}, bf16[64,5625]{1,0:T(8,128)(2,1)S(1)}, u32[]{:S(2)}, u32[]{:S(2)}) collective-permute-start(bf16[64,5625]{1,0:T(8,128)(2,1)} %bitcast.4), channel_id=1, source_target_pairs={{0,64},{64,0},{128,192},{192,128},{256,320},{320,256},{384,448},{4... | collective-permute-start | bytes 2160008 | tf_op jit(solution)/shard_map/ppermute | solution.py:71
  10.7 1.9 %collective-permute-start.3 = (bf16[64,5625]{1,0:T(8,128)(2,1)}, bf16[64,5625]{1,0:T(8,128)(2,1)S(1)}, u32[]{:S(2)}, u32[]{:S(2)}) collective-permute-start(bf16[64,5625]{1,0:T(8,128)(2,1)} %bitcast.5), channel_id=1, source_target_pairs={{0,128},{64,448},{128,0},{192,320},{256,384},{320,192},{384,256},{... | collective-permute-start | bytes 2160008 | tf_op jit(solution)/shard_map/ppermute | solution.py:67
  12.7 0.7 %add_select_fusion.1 = (s32[288]{0:T(512)S(1)}, s32[288]{0:T(512)S(1)}) fusion(s32[288]{0:T(512)} %param.8), kind=kLoop, calls=%fused_computation.8 | loop fusion | flops 3456 | bytes 3456 | tf_op jit(solution)/shard_map/jit(floor_divide)/jit(_where)/select_n | solution.py:200
  13.4 0.4 select_reduce_fusion
  13.8 0.0 copy-start.1
  13.8 0.0 copy-start.2
  13.8 6.0 %collective-permute-done.refs_2_ = bf16[64,5625]{1,0:T(8,128)(2,1)S(1)} collective-permute-done((bf16[64,5625]{1,0:T(8,128)(2,1)}, bf16[64,5625]{1,0:T(8,128)(2,1)S(1)}, u32[]{:S(2)}, u32[]{:S(2)}) %collective-permute-start) | collective-permute-done | bytes 720032 | tf_op jit(solution)/shard_map/ppermute | solution.py:67
  19.8 1.9 %collective-permute-start.1 = (bf16[64,5625]{1,0:T(8,128)(2,1)S(1)}, bf16[64,5625]{1,0:T(8,128)(2,1)S(1)}, u32[]{:S(2)}, u32[]{:S(2)}) collective-permute-start(bf16[64,5625]{1,0:T(8,128)(2,1)S(1)} %collective-permute-done.refs_2_), channel_id=1, source_target_pairs={{0,128},{64,448},{128,0},{192,320},{256,384},{320,192},{384,256},{... | collective-permute-start | bytes 2160008 | tf_op jit(solution)/shard_map/ppermute | solution.py:67
  21.7 2.7 %compare_select_fusion.rows = bf16[288,5625]{1,0:T(8,128)(2,1)S(1)} fusion(bf16[288,5625]{1,0:T(8,128)(2,1)} %param.6, s32[5625]{0:T(1024)S(1)} %dynamic_slice.7, s32[288]{0:T(512)S(1)} %xor.24), kind=kLoop, calls=%fused_computation | loop fusion | flops 3240000 | bytes 6503652 | tf_op jit(solution)/shard_map/jit(_where)/select_n | solution.py:202
  24.5 0.0 collective-permute-done.4.refs_1_
  24.5 0.0 copy-done.1
  24.5 0.0 copy-done.2
  24.5 1.9 %shard_map.56.refs_3_ = s16[64,2,1280]{2,1,0:T(2,128)(2,1)S(1)} custom-call(s32[1]{0:T(128)} %bitcast.grp, s32[64]{0:T(128)S(1)} %copy-done.2, bf16[288,5625]{1,0:T(8,128)(2,1)S(1)} %compare_select_fusion.rows, bf16[64,5625]{1,0:T(8,128)(2,1)S(1)} %bitcast.6, bf16[64,5625]{1,0:T(8,128)(2,1)S(1)} %collective-permute-done.4.refs_1_, ...), custom_call_target="tpu_custom_call" | custom-call | flops 2488320000 | bytes 5400000 | tf_op jit(solution)/shard_map/pallas_call | solution.py:145
  26.4 0.0 collective-permute-done.3.refs_0_
  26.4 1.9 %collective-permute-start.5 = (bf16[64,5625]{1,0:T(8,128)(2,1)S(1)}, bf16[64,5625]{1,0:T(8,128)(2,1)S(1)}, u32[]{:S(2)}, u32[]{:S(2)}) collective-permute-start(bf16[64,5625]{1,0:T(8,128)(2,1)S(1)} %collective-permute-done.refs_2_), channel_id=1, source_target_pairs={{0,64},{64,0},{128,192},{192,128},{256,320},{320,256},{384,448},{4... | collective-permute-start | bytes 2160008 | tf_op jit(solution)/shard_map/ppermute | solution.py:71
  28.3 2.4 %collective-permute-start.6 = (bf16[64,5625]{1,0:T(8,128)(2,1)S(1)}, bf16[64,5625]{1,0:T(8,128)(2,1)S(1)}, u32[]{:S(2)}, u32[]{:S(2)}) collective-permute-start(bf16[64,5625]{1,0:T(8,128)(2,1)S(1)} %collective-permute-done.3.refs_0_), channel_id=1, source_target_pairs={{0,64},{64,0},{128,192},{192,128},{256,320},{320,256},{384,448},{4... | collective-permute-start | bytes 2160008 | tf_op jit(solution)/shard_map/ppermute | solution.py:71
  30.8 2.2 %collective-permute-done.1.refs_0_ = bf16[64,5625]{1,0:T(8,128)(2,1)S(1)} collective-permute-done((bf16[64,5625]{1,0:T(8,128)(2,1)S(1)}, bf16[64,5625]{1,0:T(8,128)(2,1)S(1)}, u32[]{:S(2)}, u32[]{:S(2)}) %collective-permute-start.1) | collective-permute-done | bytes 720032 | tf_op jit(solution)/shard_map/ppermute | solution.py:67
  33.0 1.9 %collective-permute-start.2 = (bf16[64,5625]{1,0:T(8,128)(2,1)S(1)}, bf16[64,5625]{1,0:T(8,128)(2,1)S(1)}, u32[]{:S(2)}, u32[]{:S(2)}) collective-permute-start(bf16[64,5625]{1,0:T(8,128)(2,1)S(1)} %collective-permute-done.1.refs_0_), channel_id=1, source_target_pairs={{0,64},{64,0},{128,192},{192,128},{256,320},{320,256},{384,448},{4... | collective-permute-start | bytes 2160008 | tf_op jit(solution)/shard_map/ppermute | solution.py:71
  34.9 0.0 collective-permute-done.5.refs_1_
  34.9 0.0 collective-permute-done.6.refs_2_
  34.9 1.9 %shard_map.57.refs_2_ = s16[64,2,1280]{2,1,0:T(2,128)(2,1)S(1)} custom-call(s32[1]{0:T(128)} %bitcast.grp, s32[64]{0:T(128)S(1)} %copy-done.2, bf16[288,5625]{1,0:T(8,128)(2,1)S(1)} %compare_select_fusion.rows, bf16[64,5625]{1,0:T(8,128)(2,1)S(1)} %collective-permute-done.3.refs_0_, ...), custom_call_target="tpu_custom_call", output_to_operand_aliasing={{}: (6, {})} | custom-call | flops 2488320000 | bytes 5400000 | tf_op jit(solution)/shard_map/pallas_call | solution.py:145
  36.8 0.2 collective-permute-done.2.refs_1_
  37.0 1.9 %shard_map.58 = s16[64,2,1280]{2,1,0:T(2,128)(2,1)S(1)} custom-call(s32[1]{0:T(128)} %bitcast.grp, s32[64]{0:T(128)S(1)} %copy-done.2, bf16[288,5625]{1,0:T(8,128)(2,1)S(1)} %compare_select_fusion.rows, bf16[64,5625]{1,0:T(8,128)(2,1)S(1)} %collective-permute-done.1.refs_0_, ...), custom_call_target="tpu_custom_call", output_to_operand_aliasing={{}: (5, {})} | custom-call | flops 1658880000 | bytes 4680000 | tf_op jit(solution)/shard_map/pallas_call | solution.py:145
  38.9 29.3 %all_to_all.5.received = s16[64,2,1280]{2,1,0:T(2,128)(2,1)S(1)} all-to-all(s16[64,2,1280]{2,1,0:T(2,128)(2,1)S(1)} %shard_map.58), channel_id=1, replica_groups={{0,41,18,59,36,13,54,31,8,49,26,3,44,21,62,39,16,57,34,11,52,29,6,47,24..., dimensions={0} | all-to-all | bytes 655360 | tf_op jit(solution)/shard_map/all_to_all | solution.py:211
  68.2 0.8 %shard_map.59 = f32[8,288]{1,0:T(8,128)} custom-call(s16[64,2,1280]{2,1,0:T(2,128)(2,1)S(1)} %all_to_all.5.received), custom_call_target="tpu_custom_call" | custom-call | tf_op jit(solution)/shard_map/pallas_call | solution.py:179
  (2 shorter events, 0.0 us)
Async XLA Ops:
  0.0 19.8 %collective-permute-start = (bf16[64,5625]{1,0:T(8,128)(2,1)}, bf16[64,5625]{1,0:T(8,128)(2,1)S(1)}, u32[]{:S(2)}, u32[]{:S(2)}) collective-permute-start(bf16[64,5625]{1,0:T(8,128)(2,1)} %bitcast.3), channel_id=1, source_target_pairs={{0,384},{64,192},{128,256},{192,64},{256,128},{320,448},{384,0},{4... | collective-permute-start | bytes 2160008 | tf_op jit(solution)/shard_map/ppermute | solution.py:67
  7.8 0.7 copy-start
  8.8 15.6 %collective-permute-start.4 = (bf16[64,5625]{1,0:T(8,128)(2,1)}, bf16[64,5625]{1,0:T(8,128)(2,1)S(1)}, u32[]{:S(2)}, u32[]{:S(2)}) collective-permute-start(bf16[64,5625]{1,0:T(8,128)(2,1)} %bitcast.4), channel_id=1, source_target_pairs={{0,64},{64,0},{128,192},{192,128},{256,320},{320,256},{384,448},{4... | collective-permute-start | bytes 2160008 | tf_op jit(solution)/shard_map/ppermute | solution.py:71
  10.7 15.7 %collective-permute-start.3 = (bf16[64,5625]{1,0:T(8,128)(2,1)}, bf16[64,5625]{1,0:T(8,128)(2,1)S(1)}, u32[]{:S(2)}, u32[]{:S(2)}) collective-permute-start(bf16[64,5625]{1,0:T(8,128)(2,1)} %bitcast.5), channel_id=1, source_target_pairs={{0,128},{64,448},{128,0},{192,320},{256,384},{320,192},{384,256},{... | collective-permute-start | bytes 2160008 | tf_op jit(solution)/shard_map/ppermute | solution.py:67
  13.8 10.7 %copy-start.1 = (bf16[5625,64]{0,1:T(8,128)(2,1)S(1)}, bf16[5625,64]{0,1:T(8,128)(2,1)}, u32[]{:S(2)}) copy-start(bf16[5625,64]{0,1:T(8,128)(2,1)} %param.5) | copy-start | bytes 2160004
  13.8 10.7 %copy-start.2 = (s32[64]{0:T(128)S(1)}, s32[64]{0:T(128)}, u32[]{:S(2)}) copy-start(s32[64]{0:T(128)} %slot_pair.5) | copy-start | bytes 772
  19.8 13.2 %collective-permute-start.1 = (bf16[64,5625]{1,0:T(8,128)(2,1)S(1)}, bf16[64,5625]{1,0:T(8,128)(2,1)S(1)}, u32[]{:S(2)}, u32[]{:S(2)}) collective-permute-start(bf16[64,5625]{1,0:T(8,128)(2,1)S(1)} %collective-permute-done.refs_2_), channel_id=1, source_target_pairs={{0,128},{64,448},{128,0},{192,320},{256,384},{320,192},{384,256},{... | collective-permute-start | bytes 2160008 | tf_op jit(solution)/shard_map/ppermute | solution.py:67
  26.4 8.5 %collective-permute-start.5 = (bf16[64,5625]{1,0:T(8,128)(2,1)S(1)}, bf16[64,5625]{1,0:T(8,128)(2,1)S(1)}, u32[]{:S(2)}, u32[]{:S(2)}) collective-permute-start(bf16[64,5625]{1,0:T(8,128)(2,1)S(1)} %collective-permute-done.refs_2_), channel_id=1, source_target_pairs={{0,64},{64,0},{128,192},{192,128},{256,320},{320,256},{384,448},{4... | collective-permute-start | bytes 2160008 | tf_op jit(solution)/shard_map/ppermute | solution.py:71
  28.3 6.5 %collective-permute-start.6 = (bf16[64,5625]{1,0:T(8,128)(2,1)S(1)}, bf16[64,5625]{1,0:T(8,128)(2,1)S(1)}, u32[]{:S(2)}, u32[]{:S(2)}) collective-permute-start(bf16[64,5625]{1,0:T(8,128)(2,1)S(1)} %collective-permute-done.3.refs_0_), channel_id=1, source_target_pairs={{0,64},{64,0},{128,192},{192,128},{256,320},{320,256},{384,448},{4... | collective-permute-start | bytes 2160008 | tf_op jit(solution)/shard_map/ppermute | solution.py:71
  33.0 4.1 %collective-permute-start.2 = (bf16[64,5625]{1,0:T(8,128)(2,1)S(1)}, bf16[64,5625]{1,0:T(8,128)(2,1)S(1)}, u32[]{:S(2)}, u32[]{:S(2)}) collective-permute-start(bf16[64,5625]{1,0:T(8,128)(2,1)S(1)} %collective-permute-done.1.refs_0_), channel_id=1, source_target_pairs={{0,64},{64,0},{128,192},{192,128},{256,320},{320,256},{384,448},{4... | collective-permute-start | bytes 2160008 | tf_op jit(solution)/shard_map/ppermute | solution.py:71
